TPU v7x, 32 devices: a whole 2x2x4 slice. The times are simulated.
32 devices in a mesh: mesh: 2 (over core), blk: 16 (over z, y, x).
Axes of the slice: x: 2, y: 2, z: 4, core: 2. Of those that a mesh axis runs over, the one named last changes fastest.
Arguments:
- rotation_step: int32 [1], replicated, may hold values from 1 to 7
- field_state: float32 [2, 16, 4, 128, 256], P('mesh', 'blk'), may hold values from -6 to 6
- diffusivity: float32 [2, 16, 2, 128, 256], P('mesh', 'blk'), may hold values from 0.05 to 2
- stretch: float32 [2, 16, 128, 256], P('mesh', 'blk'), may hold values from 100 to 3000
- donor_base: int32 [2, 16, 4096], P('mesh', 'blk'), may hold values from 0 to 32478, as said below
- donor_frac: float32 [2, 16, 3, 4096], P('mesh', 'blk'), may hold values from 0 to 1
- fringe_cell: int32 [2, 16, 4096], P('mesh', 'blk'), may hold values from 0 to 32768, as said below
Outputs:
- new_fields: float32 [2, 16, 4, 128, 256], P('mesh', 'blk')
Inputs may be any that keep to these rules, and one draw needn't show every extreme that they name: `donor_base`: each entry is z * 8 * 32 + x * 32 + y with z < 127, x < 7 and y < 31. `fringe_cell`: in each block, the slots p * 256 to (p + 1) * 256 - 1 hold the cells that receive values from block p of the other mesh, used slots first; every fringe cell of the block is named by exactly one used slot; an unused slot holds 32768. A group has 0 to 256 used slots, and in every block some group is full and some is empty.
All inputs are finite; a program needn't handle non-finite values.
Results may differ from a plain program's by a relative error of at most 0.00017.
Values sent between devices are 32-bit elements; how exact they have to be, the bound alone decides.
No kernel may reach another device: no remote copies, remote signals or barrier semaphores. Data moves between devices by JAX's collectives and lax.ppermute only.
A program may use at most 64 MiB of HBM per device.

v0:
```python
import functools
import jax
import jax.numpy as jnp
from jax import lax
from jax.experimental import pallas as pl
from jax.experimental.pallas import tpu as pltpu
from jax.sharding import PartitionSpec as P

CY = 32
ITERS = 2
TURN_MOST = 7
F32, BF = jnp.float32, jnp.bfloat16
VM = pl.BlockSpec(memory_space=pltpu.VMEM)
SM = pl.BlockSpec(memory_space=pltpu.SMEM)
ANY = pl.BlockSpec(memory_space=pl.ANY)
WHOLE = pltpu.CompilerParams(vmem_limit_bytes=64 * 1024 * 1024)
CP = pltpu.CompilerParams(vmem_limit_bytes=48 * 1024 * 1024)


def split2(v):
    hi = v.astype(BF)
    lo = (v - hi.astype(F32)).astype(BF)
    return hi, lo


def down(v, k):
    return pltpu.roll(v, k, axis=0)
def up(v, k):
    return pltpu.roll(v, v.shape[0] - k, axis=0)

def factor(g_ref, q0, q1, p1, q2, p2, h, iv):
    nz, w = g_ref.shape
    for c in range(0, w, 128):
        s = slice(c, c+128)
        z = lax.broadcasted_iota(jnp.int32, (nz, 128), 0)
        g = g_ref[:, s]
        q = 1.0 / g
        q0[:, s] = q
        qd = jnp.where(z >= 1, down(q, 1), 0.0)
        qu = jnp.where(z < nz-1, up(q, 1), 0.0)
        g = g - qd - qu
        p = jnp.where(z >= 2, qd, 0.0)
        for k, (qr, pr) in ((2, (q1, p1)), (4, (q2, p2))):
            q = 1.0 / g
            qr[:, s] = q
            pr[:, s] = p
            pq = p * q
            ppq = p * pq
            g = g - p * p * down(q, k) - up(ppq, k)
            p = p * down(pq, k)
            p = jnp.where(z >= 2*k, p, 0.0)
        g_ref[:, s] = g
        h[:, s] = p
    prev = None
    for r in range(0, nz, 8):
        g = g_ref[r:r+8, :]
        if prev is None:
            hk = jnp.zeros_like(g)
        else:
            p = h[r:r+8, :]
            hk = p * prev
            g = g - p * hk
        prev = 1.0 / g
        h[r:r+8, :] = hk
        iv[r:r+8, :] = prev

def reduce_rhs(r, s, fs):
    q0, q1, p1, q2, p2 = fs
    nz = r.shape[0]
    z = lax.broadcasted_iota(jnp.int32, r.shape, 0)
    w = q0[:, s] * r
    r = r + jnp.where(z >= 1, down(w, 1), 0.0) + jnp.where(z < nz-1, up(w, 1), 0.0)
    for k, qr, pr in ((2, q1, p1), (4, q2, p2)):
        w = qr[:, s] * r
        p = pr[:, s]
        r = r + p * down(w, k) + up(p * w, k)
    return r


def substitute(y, h, iv, widen):
    nz = y.shape[0]
    prev = y[0:8, :]
    for r in range(8, nz, 8):
        prev = y[r:r+8, :] + widen(h[r:r+8, :]) * prev
        y[r:r+8, :] = prev
    prev = prev * widen(iv[nz-8:nz, :])
    y[nz-8:nz, :] = prev
    for r in range(nz-16, -1, -8):
        prev = y[r:r+8, :] * widen(iv[r:r+8, :]) + widen(h[r+8:r+16, :]) * prev
        y[r:r+8, :] = prev


def same(v):
    return v


def lanes(nz):
    return lax.broadcasted_iota(jnp.int32, (nz, 128), 1)


def on_fringe(lane):
    return (lane % CY == 0) | (lane % CY == CY - 1)


def pack_planes(get, nf, t, x, lane):
    out = None
    for f in range(nf):
        v = get(f, t)
        by = (f - x) * CY % 128
        v = v if by == 0 else pltpu.roll(v, by, axis=1)
        out = v if out is None else jnp.where(lane >= f * CY, v, out)
    return out


def pack_kernel(f_any, kap_any, al_any, lo_ref, hi_ref, f_ref, kap_ref, al_ref, sems):
    nf, nz, npl = f_ref.shape
    copies = [pltpu.make_async_copy(f_any.at[f], f_ref.at[f], sems.at[f]) for f in range(nf)]
    copies += [pltpu.make_async_copy(kap_any.at[k], kap_ref.at[k], sems.at[nf + k]) for k in range(2)]
    copies += [pltpu.make_async_copy(al_any, al_ref, sems.at[nf + 2])]
    for c in copies:
        c.start()
    for c in copies:
        c.wait()
    lane = lanes(nz)
    per, nt = 128 // CY, npl // 128

    def field(f, t):
        return f_ref[f, :, t*128:(t+1)*128]

    def coef(f, t):
        sl = slice(t*128, (t+1)*128)
        return kap_ref[f, :, sl] if f < 2 else al_ref[:, sl]

    for ref, t, x, step in ((lo_ref, 0, 0, 1), (hi_ref, nt - 1, per - 1, -1)):
        ref[0] = pack_planes(field, nf, t, x, lane)
        ref[1] = pack_planes(field, nf, t, x + step, lane)
        ref[2] = pack_planes(coef, 3, t, x, lane)


def pack(fields, kappa, along):
    nf, nz, npl = fields.shape
    sh = jax.ShapeDtypeStruct((3, nz, nf * CY), F32)
    return pl.pallas_call(
        pack_kernel,
        out_shape=(sh, sh),
        in_specs=[ANY] * 3,
        out_specs=(VM, VM),
        scratch_shapes=[pltpu.VMEM(v.shape, F32) for v in (fields, kappa, along)] + [pltpu.SemaphoreType.DMA((nf + 3,))],
        compiler_params=WHOLE,
        name="pack",
    )(fields, kappa, along)


def places(turn, tiles, blocks, turned):
    back = lax.axis_index("mesh")
    me = lax.axis_index("blk")
    by = 0 if turned else turn * (1 - back)
    return by, tiles * (1 - back), lax.rem(me + turn * back, blocks), back, lax.rem(me + blocks - turn * back, blocks)


def load_tiles(unroll, o_ref, info_ref, base_ref, frac_ref, a_ref, shift, nf, nz, npl, tile):
    nx = npl // CY
    nt = base_ref.shape[1] // tile
    o_ref[pl.ds(nt - info_ref[1], nt)] = jnp.zeros((nt,) + o_ref.shape[1:], F32)

    def body(t, carry):
        g = t if shift is None else lax.rem(t + shift, nt)
        off = pl.multiple_of(g * tile, tile)
        b = base_ref[0:1, pl.ds(off, tile)]
        fz, fx, fy = [frac_ref[i, :, pl.ds(off, tile)] for i in range(3)]
        z0 = b // npl
        x0 = b // CY % nx
        y0 = b % CY
        iz = lax.broadcasted_iota(jnp.int32, (nz, tile), 0)
        whi, wlo = split2(jnp.where(iz == z0, 1.0 - fz, jnp.where(iz == z0 + 1, fz, 0.0)))
        w = jnp.concatenate([whi, wlo, whi, wlo], axis=0)
        iy = lax.broadcasted_iota(jnp.int32, (CY, tile), 0)
        wy = jnp.where(iy == y0, 1.0 - fy, jnp.where(iy == y0 + 1, fy, 0.0))
        wx = [jnp.where(x0 == x, 1.0 - fx, jnp.where(x0 == x - 1, fx, 0.0)) for x in range(nx)]
        rows = []
        for f in range(nf):
            p = jnp.dot(a_ref[f * npl:(f + 1) * npl, :], w, preferred_element_type=F32)
            acc = wx[0] * p[:CY]
            for x in range(1, nx):
                acc = acc + wx[x] * p[x * CY:(x + 1) * CY]
            r = jnp.sum(acc * wy, axis=0, keepdims=True)
            rows += [r[:, i * 128:(i + 1) * 128] for i in range(tile // 128)]
        o_ref[info_ref[1] + t] = jnp.concatenate(rows, axis=0)
        return carry

    lax.fori_loop(0, nt, body, 0, unroll=unroll)


def split_into(a_ref, row, v):
    n, nz = v.shape
    hi, lo = split2(v)
    for i, part in enumerate((hi, hi, lo, lo)):
        a_ref[row:row + n, i * nz:(i + 1) * nz] = part


def interp_kernel(turn_any, f_any, base_any, frac_any, o_ref, a_ref, f_ref, base_ref, frac_ref, turn_ref, sems, *, tile, blocks, turned):
    nf, nz, npl = f_ref.shape
    copies = [pltpu.make_async_copy(f_any.at[f], f_ref.at[f], sems.at[f]) for f in range(nf)]
    copies += [pltpu.make_async_copy(base_any, base_ref, sems.at[nf])]
    copies += [pltpu.make_async_copy(frac_any, frac_ref, sems.at[nf + 1])]
    copies += [pltpu.make_async_copy(turn_any, turn_ref, sems.at[nf + 2])]
    for c in copies:
        c.start()
    for f in range(nf):
        copies[f].wait()
        split_into(a_ref, f * npl, f_ref[f].T)
    for c in copies[nf:]:
        c.wait()
    info_ref = places(turn_ref[0], base_ref.shape[1] // tile, blocks, turned)
    load_tiles(16, o_ref, info_ref, base_ref, frac_ref, a_ref, info_ref[0], nf, nz, npl, tile)


def interp(turn, fields, base, frac, tile, blocks, turned):
    nf, nz, npl = fields.shape
    slots = base.shape[-1]
    return pl.pallas_call(
        functools.partial(interp_kernel, tile=tile, blocks=blocks, turned=turned),
        out_shape=jax.ShapeDtypeStruct((2 * slots // tile, nf * tile // 128, 128), F32),
        in_specs=[ANY] * 4,
        out_specs=VM,
        scratch_shapes=[pltpu.VMEM((nf * npl, 4 * nz), BF), pltpu.VMEM(fields.shape, F32),
                        pltpu.VMEM(base.shape, jnp.int32), pltpu.VMEM(frac.shape, F32),
                        pltpu.SMEM((1,), jnp.int32), pltpu.SemaphoreType.DMA((nf + 3,))],
        compiler_params=CP,
        name="interp",
    )(turn, fields, base, frac)


def right_sides(start_ref, tiles, hl, hr, kap_ref, si, y, fs, lane):
    nf, nz, npl = start_ref.shape
    nt = npl // 128
    for f in range(nf):
        k = 1 if f == nf - 1 else 0
        v = tiles(f)
        rp = [pltpu.roll(u, CY, axis=1) for u in v]
        rm = [pltpu.roll(u, 128 - CY, axis=1) for u in v]
        left_in = hl if f == 0 else pltpu.roll(hl, 128 - f * CY, axis=1)
        by = (128 - CY - f * CY) % 128
        right_in = hr if by == 0 else pltpu.roll(hr, by, axis=1)
        for t in range(nt):
            left = jnp.where(lane < CY, left_in if t == 0 else rp[t-1], rp[t])
            right = jnp.where(lane >= 128 - CY, right_in if t == nt - 1 else rm[t+1], rm[t])
            side = pltpu.roll(v[t], 1, axis=1) + pltpu.roll(v[t], 127, axis=1)
            sl = slice(t * 128, (t + 1) * 128)
            r = (start_ref[f, :, sl] + kap_ref[k, :, sl] * (left + right + side)) * si[:, sl]
            y[:, f*npl+t*128:f*npl+(t+1)*128] = reduce_rhs(r, slice(k*npl + t*128, k*npl + (t+1)*128), fs)


def march_kernel(start_ref, kap_ref, al_ref, lo_ref, hi_ref, left_ref, right_ref, cells_ref,
                 f1t_ref, pay_ref, fac_ref, y, y2, g, q0, q1, p1, q2, p2, h, iv, si, gs):
    nf, nz, npl = start_ref.shape
    nt = npl // 128
    own = 2 * npl
    lane = lanes(nz)
    fringe = on_fringe(lane)
    inv = 1.0 / al_ref[...]
    si[...] = inv
    for k in range(2):
        g[:, k*npl:(k+1)*npl] = 2.0 + (1.0 + 4.0 * kap_ref[k]) * inv
    outer = []
    for i, (near, mine) in enumerate(((left_ref, lo_ref), (right_ref, hi_ref))):
        c3 = near[2]
        r32, r64, r96 = [pltpu.roll(c3, j, axis=1) for j in (32, 64, 96)]
        c = jnp.where(lane < CY, c3, jnp.where(lane < 2*CY, r32, r64))
        s = jnp.where(lane < CY, r64, jnp.where(lane < 2*CY, r96, jnp.where(lane < 3*CY, c3, r32)))
        inv = 1.0 / s
        g[:, own+i*128:own+(i+1)*128] = 2.0 + (1.0 + 4.0 * c) * inv
        v = near[0]
        z = jnp.where(fringe, 0.0, v)
        side = pltpu.roll(z, 1, axis=1) + pltpu.roll(z, 127, axis=1)
        outer.append((v + c * (near[1] + mine[0] + side)) * inv)
    fs = (q0, q1, p1, q2, p2)
    factor(g, q0, q1, p1, q2, p2, h, iv)

    def clear(v):
        return jnp.where(fringe, 0.0, v)

    right_sides(start_ref, lambda f: [clear(start_ref[f, :, t*128:(t+1)*128]) for t in range(nt)],
                left_ref[0], right_ref[0], kap_ref, si, y, fs, lane)
    for i in range(2):
        y[:, nf*npl+i*128:nf*npl+(i+1)*128] = reduce_rhs(outer[i], slice(own+i*128, own+(i+1)*128), fs)

    def widen(v):
        m, p = v[:, :npl], v[:, npl:own]
        return jnp.concatenate([m] * (nf - 1) + [p, v[:, own:]], axis=1)

    def widen_own(v):
        m, p = v[:, :npl], v[:, npl:own]
        return jnp.concatenate([m] * (nf - 1) + [p], axis=1)

    substitute(y, h, iv, widen)

    def first(f):
        return [clear(y[:, f*npl+t*128:f*npl+(t+1)*128]) for t in range(nt)]

    right_sides(start_ref, first, y[:, nf*npl:nf*npl+128], y[:, nf*npl+128:nf*npl+256], kap_ref, si, y2, fs, lane)
    substitute(y2, h, iv, widen_own)
    for f in range(nf):
        for t in range(nt):
            j = f * nt + t
            pay_ref[j*nz:(j+1)*nz, :] = y2[:, f*npl+t*128:f*npl+(t+1)*128]
    for f in range(nf):
        v = first(f)
        for t in range(nt):
            f1t_ref[f*npl+t*128:f*npl+(t+1)*128, :] = v[t].T
    nx = npl // CY
    half = nf * 2 * nx
    ln = lane % half
    x, side, deep = ln // 2 % nx, ln % 2, jnp.where(lane >= half, 2, 1)
    src = x % (128 // CY) * CY + jnp.where(side == 0, deep, CY - 1 - deep)

    def pick(get):
        out = None
        for t in range(nt):
            v = jnp.take_along_axis(get(t), src, axis=1)
            out = v if out is None else jnp.where(x // (128 // CY) == t, v, out)
        return out

    ck = [pick(lambda t, k=k: kap_ref[k, :, t*128:(t+1)*128]) for k in range(2)]
    c = jnp.where(ln // (2 * nx) == nf - 1, ck[1], ck[0])
    inv = pick(lambda t: si[:, t*128:(t+1)*128])
    cs = c * inv
    gg = 2.0 + (inv + 4.0 * cs)
    j = nf * nt
    pay_ref[j*nz:(j+1)*nz, :] = cs
    pay_ref[(j+1)*nz:(j+2)*nz, :] = gg
    pay_ref[(j+2)*nz:, :] = cells_ref[...].astype(F32)
    gs[...] = gg
    refs = [fac_ref.at[i*nz:(i+1)*nz] for i in range(7)]
    factor(gs, *refs)
    fac_ref[7*nz:, :] = cs


def march(start, kappa, along, low, high, left, right, cells):
    nf, nz, npl = start.shape
    nt = npl // 128
    rows = (nf * nt + 2) * nz + cells.shape[0]
    w = 2 * npl + 256
    return pl.pallas_call(
        march_kernel,
        out_shape=(jax.ShapeDtypeStruct((nf * npl, nz), F32), jax.ShapeDtypeStruct((rows, 128), F32),
                   jax.ShapeDtypeStruct((8 * nz, 128), F32)),
        in_specs=[VM] * 8,
        out_specs=(VM, VM, VM),
        scratch_shapes=[pltpu.VMEM((nz, nf*npl+256), F32), pltpu.VMEM((nz, nf*npl), F32)]
        + [pltpu.VMEM((nz, w), F32)] * 8 + [pltpu.VMEM((nz, npl), F32), pltpu.VMEM((nz, 128), F32)],
        compiler_params=CP,
        name="march",
    )(start, kappa, along, low, high, left, right, cells)


def place_small(shift, arr_ref, row0, cell_row, slots, nf, nz, npl):
    rows = arr_ref.shape[1]
    per = rows // nf
    tile = per * 128
    nt = slots // tile
    nx = npl // CY
    nq = 2 * nx
    zo, av = [], []
    for t in range(nt):
        c = cell_row(lax.rem(t + shift, nt), tile)
        cz = c // npl
        q = c // CY % nx * 2 + c % 2
        zo.append((lax.broadcasted_iota(jnp.int32, (nz, tile), 0) == cz).astype(F32).astype(BF))
        oh = lax.broadcasted_iota(jnp.int32, (nq, tile), 0) == q
        a = arr_ref[row0 + t]
        his, los = [], []
        for f in range(nf):
            row = jnp.concatenate([a[f*per+i:f*per+i+1] for i in range(per)], axis=1)
            hi, lo = split2(jnp.where(oh, row, 0.0))
            his.append(hi)
            los.append(lo)
        av.append(jnp.concatenate(his + los, axis=0))
    zo = jnp.concatenate(zo, axis=1)
    av = jnp.concatenate(av, axis=1)
    return lax.dot_general(zo, av, (((1,), (1,)), ((), ())), preferred_element_type=F32)


def spots(k, nf, npl, low, high):
    nq = 2 * npl // CY
    return k // nq % nf * npl + k % nq // 2 * CY + jnp.where(k % 2 == 0, low, high)


def relay_kernel(turn_ref, arr_ref, cells_ref, f1t_ref, fac_ref, base_ref, frac_ref, o_ref, e_ref, a_ref, ys, *, tile, nf, edges, blocks, turned):
    nz = f1t_ref.shape[1]
    info_ref = places(turn_ref[0], base_ref.shape[1] // tile, blocks, turned)
    npl = f1t_ref.shape[0] // nf
    slots = base_ref.shape[1]
    half = nf * 2 * npl // CY
    lane = lanes(nz)

    def cell_row(g, tile):
        return cells_ref[0:1, pl.ds(pl.multiple_of(g * tile, tile), tile)]

    sm = place_small(info_ref[0], arr_ref, info_ref[1], cell_row, slots, nf, nz, npl)
    fr = sm + pltpu.roll(sm, half, axis=1)
    fac = [fac_ref.at[i*nz:(i+1)*nz] for i in range(8)]
    ys[...] = reduce_rhs(fac[7][...] * fr, slice(0, 128), fac[:5])
    substitute(ys, fac[5], fac[6], same)
    e = ys[...]
    e_ref[...] = e
    hi, lo = split2(e)
    both = jnp.where(lane < half, hi.astype(F32), pltpu.roll(lo.astype(F32), half, axis=1))
    terms = jnp.concatenate([sm.astype(BF), both.astype(BF)], axis=1)
    k = lax.broadcasted_iota(jnp.int32, (1, 256), 1)
    target = jnp.where(k < 128, spots(k, nf, npl, 0, CY - 1), spots(k, nf, npl, 1, CY - 2))
    for f in range(nf):
        row = lax.broadcasted_iota(jnp.int32, (npl, 256), 0) + f * npl
        put = (row == target).astype(F32).astype(BF)
        add = lax.dot_general(put, terms, (((1,), (1,)), ((), ())), preferred_element_type=F32)
        split_into(a_ref, f * npl, f1t_ref[f*npl:(f+1)*npl, :] + add)
    load_tiles(UNROLL, o_ref, info_ref, base_ref, frac_ref, a_ref, None, nf, nz, npl, tile)
    if edges:
        turned = e.T
        nt = slots // tile
        nq = half // nf
        for col, by in ((nq - 2, 1), (0, nt - 1)):
            rows = jnp.concatenate([turned[f*nq+col:f*nq+col+2] for f in range(nf)], axis=0)
            o_ref[nt - info_ref[1] + lax.rem(info_ref[2] + by, nt)] = rows


def relay(turn, arrived, cells, f1t, fac, base, frac, tile, nf, edges, blocks, turned):
    nz = f1t.shape[1]
    return pl.pallas_call(
        functools.partial(relay_kernel, tile=tile, nf=nf, edges=edges, blocks=blocks, turned=turned),
        out_shape=(jax.ShapeDtypeStruct(arrived.shape, F32), jax.ShapeDtypeStruct((nz, 128), F32)),
        in_specs=[SM] + [VM] * 6,
        out_specs=(VM, VM),
        scratch_shapes=[pltpu.VMEM((f1t.shape[0], 4 * nz), BF), pltpu.VMEM((nz, 128), F32)],
        compiler_params=CP,
        name="relay",
    )(turn, arrived, cells, f1t, fac, base, frac)


def finish_kernel(turn_ref, arr_ref, own_ref, moved_ref, e_ref, came_ref, *rest, edges, blocks, turned):
    if edges:
        o_ref, pay_ref, ys, gs, *fac, sems = rest
    else:
        el_ref, er_ref, o_ref, pay_ref, ys, gs, *fac, sems = rest
    nf, nz, npl = o_ref.shape
    nt = npl // 128
    nx = npl // CY
    nq = 2 * nx
    half = nf * nq
    j = nf * nt
    cells0 = (j + 2) * nz
    slots = (pay_ref.shape[0] - cells0) * 128
    info_ref = places(turn_ref[0], arr_ref.shape[0] // 2, blocks, turned)

    lines = slice(j * nz, pay_ref.shape[0])
    rest = slice(0, j * nz)

    def copies(ref):
        return [pltpu.make_async_copy(ref.at[s], pay_ref.at[s], sems.at[i]) for i, s in enumerate((lines, rest))]

    @pl.when(info_ref[3] == 0)
    def _():
        for c in copies(own_ref):
            c.start()

    @pl.when(info_ref[3] != 0)
    def _():
        for c in copies(moved_ref):
            c.start()

    lane = lanes(nz)
    q = lane % nq
    e = jnp.where(info_ref[3] == 0, e_ref[...], came_ref[...])
    if edges:
        chunks = arr_ref.shape[0] // 2
        el = arr_ref[chunks - info_ref[1] + lax.rem(info_ref[4] + chunks - 1, chunks)]
        er = arr_ref[chunks - info_ref[1] + lax.rem(info_ref[4] + 1, chunks)]
        none = jnp.zeros((nq - 4, nz), F32)
        parts = []
        for f in range(nf):
            parts += [el[2*f:2*f+2], none, er[2*f:2*f+2]]
        parts = jnp.concatenate(parts, axis=0)
        outer = jnp.concatenate([parts, parts], axis=0).T
        left = right = outer
    else:
        left = pltpu.roll(el_ref[...], 128 - (nq - 2), axis=1)
        right = pltpu.roll(er_ref[...], nq - 2, axis=1)
    left = jnp.where(q < 2, left, pltpu.roll(e, 2, axis=1))
    right = jnp.where(q >= nq - 2, right, pltpu.roll(e, 126, axis=1))
    deep = pltpu.roll(e, half, axis=1)
    copies(own_ref)[0].wait()
    gs[...] = pay_ref[(j+1)*nz:(j+2)*nz, :]
    factor(gs, *fac)

    def cell_row(g, tile):
        per = tile // 128
        rows = [pay_ref[pl.ds(cells0 + g * per + i, 1), :] for i in range(per)]
        return jnp.concatenate(rows, axis=1).astype(jnp.int32)

    sm = place_small(info_ref[0], arr_ref, info_ref[1], cell_row, slots, nf, nz, npl)
    fr = sm + pltpu.roll(sm, half, axis=1)
    cs = pay_ref[j*nz:(j+1)*nz, :]
    r = cs * jnp.where(lane < half, fr + left + right, deep)
    ys[...] = reduce_rhs(r, slice(0, 128), fac[:5])
    substitute(ys, fac[5], fac[6], same)
    hi, lo = split2(ys[...])
    terms = jnp.concatenate([sm.astype(BF), hi, lo], axis=1)
    k = lax.broadcasted_iota(jnp.int32, (384, 1), 0)
    near = jnp.where(k % 128 < half, 1, 2)
    target = jnp.where(k < 128, spots(k, nf, npl, 0, CY - 1), spots(k, nf, npl, near, CY - 1 - near))
    fringe = on_fringe(lane)
    copies(own_ref)[1].wait()
    for f in range(nf):
        put = (lax.broadcasted_iota(jnp.int32, (384, npl), 1) + f * npl == target).astype(F32).astype(BF)
        add = jnp.dot(terms, put, preferred_element_type=F32)
        for t in range(nt):
            v = pay_ref[(f*nt+t)*nz:(f*nt+t+1)*nz, :]
            o_ref[f, :, t*128:(t+1)*128] = jnp.where(fringe, 0.0, v) + add[:, t*128:(t+1)*128]


def finish(turn, shape, arrived, own, moved, e, blocks, turned):
    nz = shape[1]
    return pl.pallas_call(
        functools.partial(finish_kernel, edges=len(e) == 2, blocks=blocks, turned=turned),
        out_shape=jax.ShapeDtypeStruct(shape, F32),
        in_specs=[SM, VM, ANY, ANY] + [VM] * len(e),
        out_specs=VM,
        scratch_shapes=[pltpu.VMEM(own.shape, F32)] + [pltpu.VMEM((nz, 128), F32)] * 9 + [pltpu.SemaphoreType.DMA((2,))],
        compiler_params=CP,
        name="finish",
    )(turn, arrived, own, moved, *e)


TILE = 256
UNROLL = 4


def exchange(values, blocks, cap, nf):
    if cap == TILE:
        return lax.all_to_all(values, ("mesh", "blk"), 0, 0, tiled=True)
    halves = values.reshape(2, -1, nf, TILE).transpose(0, 2, 1, 3).reshape(2, nf, blocks, cap)
    sent = halves.transpose(0, 2, 1, 3).reshape(2 * blocks, nf, cap)
    got = lax.all_to_all(sent, ("mesh", "blk"), 0, 0, tiled=True)
    got = got.reshape(2, blocks, nf, cap).transpose(0, 2, 1, 3).reshape(2, nf, -1, TILE)
    return got.transpose(0, 2, 1, 3).reshape(values.shape)


def turn(values, cap, by):
    groups = values.reshape(values.shape[:-1] + (-1, cap))
    return jnp.roll(groups, -by, axis=-2).reshape(values.shape)


def local(rotation_step, field_state, diffusivity, stretch, donor_base, donor_frac, fringe_cell):
    on_back = lax.axis_index("mesh") == 1
    blocks = lax.axis_size("blk")
    rotation = rotation_step[0]
    start, kappa, along = field_state[0, 0], diffusivity[0, 0], stretch[0, 0]
    base, frac, cells = donor_base[0, 0], donor_frac[0, 0], fringe_cell[0, 0]
    nf = start.shape[0]
    slots = base.shape[0]
    cap = slots // blocks
    turned = cap != TILE
    send0, frac0, cells0 = base, frac, cells
    if turned:
        by = jnp.where(on_back, 0, rotation)
        send0, frac0, cells0 = turn(base, cap, by), turn(frac, cap, by), turn(cells, cap, by)
    edges = cap == TILE and 2 * nf == nf * TILE // 128
    row = (1, slots)
    low, high = pack(start, kappa, along)
    left = lax.ppermute(high, "blk", [(i, (i + 1) % blocks) for i in range(blocks)])
    right = lax.ppermute(low, "blk", [((i + 1) % blocks, i) for i in range(blocks)])
    values = interp(rotation_step, start, send0.reshape(row), frac0.reshape(3, 1, slots), TILE, blocks, turned)

    def branch(distance):
        def shift(v, off, blade):
            pairs = [(i, (i + off) % blocks) for i in range(blocks)] if blade else []
            pairs = pairs + [(blocks + i, blocks + (i + distance + off) % blocks) for i in range(blocks)]
            return lax.ppermute(v, ("mesh", "blk"), pairs)

        def run(pay, step, arrived, f1t, fac, base, frac, cells0):
            moved = shift(pay, 0, False)
            values, e = relay(
                step, arrived, cells0.reshape(row), f1t, fac, base.reshape(row), frac.reshape(3, 1, slots), TILE, nf, edges,
                blocks, turned,
            )
            arrived = exchange(values, blocks, cap, nf)
            near = () if edges else (shift(e, 1, True), shift(e, -1, True))
            return arrived, moved, e, shift(e, 0, False), *near

        return run

    values, left, right = lax.optimization_barrier((values, left, right))
    arrived = exchange(values, blocks, cap, nf)
    f1t, pay, fac = march(start, kappa, along, low, high, left, right, cells0.reshape(-1, 128))
    arrived, moved, e, came, *near = lax.switch(
        rotation - 1, [branch(d) for d in range(1, TURN_MOST + 1)], pay, rotation_step, arrived, f1t, fac, base, frac, cells0
    )
    return finish(rotation_step, start.shape, arrived, pay, moved, (e, came, *near), blocks, turned)[None, None]


def solution(mesh):
    placed = (
        P(),
        P("mesh", "blk", None, None, None),
        P("mesh", "blk", None, None, None),
        P("mesh", "blk", None, None),
        P("mesh", "blk", None),
        P("mesh", "blk", None, None),
        P("mesh", "blk", None),
    )
    return jax.shard_map(
        local,
        mesh=mesh,
        in_specs=placed,
        out_specs=P("mesh", "blk", None, None, None),
        check_vma=False,
    )
```

profile of v0, /device:TPU:1, one launch (start us, length us, event | category | flops | bytes accessed | tf_op | source)
XLA Modules:
  0.0 54.7 jit_solution(2409732544191856140)
XLA Ops:
  0.0 2.3 %pack.1 = (f32[3,128,128]{2,1,0:T(8,128)}, f32[3,128,128]{2,1,0:T(8,128)}) custom-call(f32[4,128,256]{2,1,0:T(8,128)} %bitcast.43, f32[2,128,256]{2,1,0:T(8,128)} %bitcast.46, f32[128,256]{1,0:T(8,128)} %bitcast.48), custom_call_target="tpu_custom_call" | custom-call | tf_op jit(solution)/shard_map/pack/pallas_call | solution.py:143
  2.3 2.1 %collective-permute-start.14 = (f32[3,128,128]{2,1,0:T(8,128)}, f32[3,128,128]{2,1,0:T(8,128)S(1)}, u32[]{:S(2)}, u32[]{:S(2)}) collective-permute-start(f32[3,128,128]{2,1,0:T(8,128)} %get-tuple-element.199.hi_ref), channel_id=1, source_target_pairs={{0,1},{1,2},{2,3},{3,4},{4,5},{5,6},{6,7},{7,8},{8,9},{9,10},{10,1... | collective-permute-start | bytes 589832 | tf_op jit(solution)/shard_map/ppermute | solution.py:570
  4.4 4.1 %collective-permute-start.15 = (f32[3,128,128]{2,1,0:T(8,128)}, f32[3,128,128]{2,1,0:T(8,128)S(1)}, u32[]{:S(2)}, u32[]{:S(2)}) collective-permute-start(f32[3,128,128]{2,1,0:T(8,128)} %get-tuple-element.200.lo_ref), channel_id=1, source_target_pairs={{1,0},{2,1},{3,2},{4,3},{5,4},{6,5},{7,6},{8,7},{9,8},{10,9},{11,1... | collective-permute-start | bytes 589832 | tf_op jit(solution)/shard_map/ppermute | solution.py:571
  9.1 0.0 copy-start
  9.2 1.0 %copy-done = f32[1,1,4,128,256]{4,3,2,1,0:T(8,128)S(1)} copy-done((f32[1,1,4,128,256]{4,3,2,1,0:T(8,128)S(1)}, f32[1,1,4,128,256]{4,3,2,1,0:T(8,128)}, u32[]{:S(2)}) %copy-start) | copy-done | bytes 524312
  10.2 0.0 copy-start.1
  10.2 0.0 copy-start.3
  10.2 0.0 copy-start.7
  10.2 6.8 %interp.1 = f32[32,8,128]{2,1,0:T(8,128)} custom-call(s32[1]{0:T(128)S(6)} %copy.43.turn_any.turn_ref, f32[4,128,256]{2,1,0:T(8,128)S(1)} %bitcast.44, s32[1,4096]{1,0:T(1,128)} %bitcast.66, f32[3,1,4096]{2,1,0:T(1,128)} %bitcast.50), custom_call_target="tpu_custom_call" | custom-call | tf_op jit(solution)/shard_map/interp/pallas_call | solution.py:221
  17.0 0.0 copy-start.2
  17.0 0.0 collective-permute-done.14.left_ref
  17.0 0.0 collective-permute-done.15.right_ref
  17.0 3.5 %all-to-all-start.7 = ((f32[32,8,128]{2,1,0:T(8,128)}), f32[32,8,128]{2,1,0:T(8,128)S(1)}, u32[]{:S(2)}, u32[]{:S(2)}) async-start(f32[32,8,128]{2,1,0:T(8,128)} %interp.1), calls=%async_computation.7 | async-start | bytes 262144 | tf_op jit(solution)/shard_map/all_to_all | solution.py:540
  20.6 0.0 copy-done.1
  20.6 0.0 copy-done.3
  20.6 0.0 copy-done.7
  20.6 0.0 copy-done.2
  20.6 0.0 copy-start.4
  20.6 0.9 %copy-done.4 = f32[3,128,128]{2,1,0:T(8,128)S(1)} copy-done((f32[3,128,128]{2,1,0:T(8,128)S(1)}, f32[3,128,128]{2,1,0:T(8,128)}, u32[]{:S(2)}) %copy-start.4) | copy-done | bytes 196632
  21.5 0.0 copy-start.5
  21.5 0.9 %copy-done.5 = f32[3,128,128]{2,1,0:T(8,128)S(1)} copy-done((f32[3,128,128]{2,1,0:T(8,128)S(1)}, f32[3,128,128]{2,1,0:T(8,128)}, u32[]{:S(2)}) %copy-start.5) | copy-done | bytes 196632
  22.5 0.0 copy-start.6
  22.5 0.0 copy-start.8
  22.5 3.4 %march.1 = (f32[1024,128]{1,0:T(8,128)S(1)}, f32[1312,128]{1,0:T(8,128)S(1)}, f32[1024,128]{1,0:T(8,128)S(1)}) custom-call(f32[4,128,256]{2,1,0:T(8,128)S(1)} %bitcast.45, f32[2,128,256]{2,1,0:T(8,128)S(1)} %bitcast.47, f32[128,256]{1,0:T(8,128)S(1)} %bitcast.49, f32[3,128,128]{2,1,0:T(8,128)S(1)} %copy-done.4, f32[3,128,128]{2,1,0:T(8,128)S(1)} %copy-done.5, ...), custom_call_target="tpu_custom_call" | custom-call | tf_op jit(solution)/shard_map/march/pallas_call | solution.py:344
  25.9 2.3 %all-to-all-done.7 = f32[32,8,128]{2,1,0:T(8,128)S(1)} async-done(((f32[32,8,128]{2,1,0:T(8,128)}), f32[32,8,128]{2,1,0:T(8,128)S(1)}, u32[]{:S(2)}, u32[]{:S(2)}) %all-to-all-start.7) | async-done | bytes 131104 | tf_op jit(solution)/shard_map/all_to_all | solution.py:540
  28.2 0.0 copy-done.6
  28.2 0.0 copy-done.8
  28.2 22.2 %conditional.1 = (f32[32,8,128]{2,1,0:T(8,128)}, f32[1312,128]{1,0:T(8,128)}, f32[128,128]{1,0:T(8,128)}, f32[128,128]{1,0:T(8,128)}) conditional(s32[]{:T(128)} %bitcast.35, (s32[1,1,4096]{2,1,0:T(1,128)S(1)}, s32[1,1,4096]{2,1,0:T(1,128)S(1)}, f32[1,1,3,4096]{3,1,2,0:T(1,128)S(1)}, s32[1]{0:T(128)}, ...), branch_computations={%region_0.0_spmd, %region_1.0_spmd, %region_2.0_spmd, %region_3.0_... | conditional | bytes 3342480 | solution.py:595
  28.2 2.6 %collective-permute-start.6 = (f32[1312,128]{1,0:T(8,128)S(1)}, f32[1312,128]{1,0:T(8,128)}, u32[]{:S(2)}, u32[]{:S(2)}) collective-permute-start(f32[1312,128]{1,0:T(8,128)S(1)} %get-tuple-element.155), channel_id=1, source_target_pairs={{16,20},{17,21},{18,22},{19,23},{20,24},{21,25},{22,26},{23,27},{2... | collective-permute-start | bytes 2015240 | tf_op jit(solution)/shard_map/cond/branch_3_fun/ppermute | solution.py:578
  30.8 7.9 %relay.10 = (f32[32,8,128]{2,1,0:T(8,128)}, f32[128,128]{1,0:T(8,128)}) custom-call(s32[1]{0:T(128)} %get-tuple-element.147.turn_ref, f32[32,8,128]{2,1,0:T(8,128)S(1)} %get-tuple-element.148.arr_ref, s32[1,4096]{1,0:T(1,128)S(1)} %bitcast.62, f32[1024,128]{1,0:T(8,128)S(1)} %get-tuple-element.150.f1t_ref, f32[1024,128]{1,0:T(8,128)S(1)} %get-tuple-element.151.fac_ref, ...), custom_call_target="tpu_custom_call" | custom-call | tf_op jit(solution)/shard_map/cond/branch_3_fun/relay/pallas_call | solution.py:429
  38.7 4.0 %all-to-all-start.3 = ((f32[32,8,128]{2,1,0:T(8,128)}), f32[32,8,128]{2,1,0:T(8,128)}, u32[]{:S(2)}, u32[]{:S(2)}) async-start(f32[32,8,128]{2,1,0:T(8,128)} %get-tuple-element.154), calls=%async_computation.3 | async-start | bytes 262144 | tf_op jit(solution)/shard_map/cond/branch_3_fun/all_to_all | solution.py:540
  42.7 3.3 %collective-permute-start.7 = (f32[128,128]{1,0:T(8,128)}, f32[128,128]{1,0:T(8,128)}, u32[]{:S(2)}, u32[]{:S(2)}) collective-permute-start(f32[128,128]{1,0:T(8,128)} %get-tuple-element.281), channel_id=1, source_target_pairs={{16,20},{17,21},{18,22},{19,23},{20,24},{21,25},{22,26},{23,27},{2... | collective-permute-start | bytes 196616 | tf_op jit(solution)/shard_map/cond/branch_3_fun/ppermute | solution.py:578
  46.0 4.1 %collective-permute-done.7 = f32[128,128]{1,0:T(8,128)} collective-permute-done((f32[128,128]{1,0:T(8,128)}, f32[128,128]{1,0:T(8,128)}, u32[]{:S(2)}, u32[]{:S(2)}) %collective-permute-start.7) | collective-permute-done | bytes 65568 | tf_op jit(solution)/shard_map/cond/branch_3_fun/ppermute | solution.py:578
  50.1 0.2 all-to-all-done.3
  50.3 0.0 collective-permute-done.6
  50.3 4.1 %finish.1 = f32[4,128,256]{2,1,0:T(8,128)} custom-call(s32[1]{0:T(128)S(6)} %copy.43.turn_any.turn_ref, f32[32,8,128]{2,1,0:T(8,128)} %get-tuple-element.207.arr_ref, f32[1312,128]{1,0:T(8,128)S(1)} %get-tuple-element.206.own_ref, f32[1312,128]{1,0:T(8,128)} %get-tuple-element.208.moved_ref, f32[128,128]{1,0:T(8,128)} %get-tuple-element.209.e_ref, ...), custom_call_target="tpu_custom_call" | custom-call | tf_op jit(solution)/shard_map/finish/pallas_call | solution.py:523
Async XLA Ops:
  2.3 14.7 %collective-permute-start.14 = (f32[3,128,128]{2,1,0:T(8,128)}, f32[3,128,128]{2,1,0:T(8,128)S(1)}, u32[]{:S(2)}, u32[]{:S(2)}) collective-permute-start(f32[3,128,128]{2,1,0:T(8,128)} %get-tuple-element.199.hi_ref), channel_id=1, source_target_pairs={{0,1},{1,2},{2,3},{3,4},{4,5},{5,6},{6,7},{7,8},{8,9},{9,10},{10,1... | collective-permute-start | bytes 589832 | tf_op jit(solution)/shard_map/ppermute | solution.py:570
  4.4 12.6 %collective-permute-start.15 = (f32[3,128,128]{2,1,0:T(8,128)}, f32[3,128,128]{2,1,0:T(8,128)S(1)}, u32[]{:S(2)}, u32[]{:S(2)}) collective-permute-start(f32[3,128,128]{2,1,0:T(8,128)} %get-tuple-element.200.lo_ref), channel_id=1, source_target_pairs={{1,0},{2,1},{3,2},{4,3},{5,4},{6,5},{7,6},{8,7},{9,8},{10,9},{11,1... | collective-permute-start | bytes 589832 | tf_op jit(solution)/shard_map/ppermute | solution.py:571
  9.1 1.0 %copy-start = (f32[1,1,4,128,256]{4,3,2,1,0:T(8,128)S(1)}, f32[1,1,4,128,256]{4,3,2,1,0:T(8,128)}, u32[]{:S(2)}) copy-start(f32[1,1,4,128,256]{4,3,2,1,0:T(8,128)} %param.15) | copy-start | bytes 1572868
  10.2 10.4 %copy-start.1 = (f32[1,1,4,128,256]{4,3,2,1,0:T(8,128)S(1)}, f32[1,1,4,128,256]{4,3,2,1,0:T(8,128)}, u32[]{:S(2)}) copy-start(f32[1,1,4,128,256]{4,3,2,1,0:T(8,128)} %param.15) | copy-start | bytes 1572868
  10.2 10.4 %copy-start.3 = (f32[1,1,128,256]{3,2,1,0:T(8,128)S(1)}, f32[1,1,128,256]{3,2,1,0:T(8,128)}, u32[]{:S(2)}) copy-start(f32[1,1,128,256]{3,2,1,0:T(8,128)} %param.17) | copy-start | bytes 393220
  10.2 10.4 %copy-start.7 = (s32[1,1,4096]{2,1,0:T(1,128)S(1)}, s32[1,1,4096]{2,1,0:T(1,128)}, u32[]{:S(2)}) copy-start(s32[1,1,4096]{2,1,0:T(1,128)} %param.20) | copy-start | bytes 49156
  17.0 3.6 %copy-start.2 = (f32[1,1,2,128,256]{4,3,2,1,0:T(8,128)S(1)}, f32[1,1,2,128,256]{4,3,2,1,0:T(8,128)}, u32[]{:S(2)}) copy-start(f32[1,1,2,128,256]{4,3,2,1,0:T(8,128)} %param.16) | copy-start | bytes 786436
  17.0 11.1 %all-to-all-start.7 = ((f32[32,8,128]{2,1,0:T(8,128)}), f32[32,8,128]{2,1,0:T(8,128)S(1)}, u32[]{:S(2)}, u32[]{:S(2)}) async-start(f32[32,8,128]{2,1,0:T(8,128)} %interp.1), calls=%async_computation.7 | async-start | bytes 262144 | tf_op jit(solution)/shard_map/all_to_all | solution.py:540
  20.6 0.9 %copy-start.4 = (f32[3,128,128]{2,1,0:T(8,128)S(1)}, f32[3,128,128]{2,1,0:T(8,128)}, u32[]{:S(2)}) copy-start(f32[3,128,128]{2,1,0:T(8,128)} %get-tuple-element.200.lo_ref) | copy-start | bytes 589828
  21.5 0.9 %copy-start.5 = (f32[3,128,128]{2,1,0:T(8,128)S(1)}, f32[3,128,128]{2,1,0:T(8,128)}, u32[]{:S(2)}) copy-start(f32[3,128,128]{2,1,0:T(8,128)} %get-tuple-element.199.hi_ref) | copy-start | bytes 589828
  22.5 5.7 %copy-start.6 = (f32[1,1,3,4096]{3,1,2,0:T(1,128)S(1)}, f32[1,1,3,4096]{3,1,2,0:T(1,128)}, u32[]{:S(2)}) copy-start(f32[1,1,3,4096]{3,1,2,0:T(1,128)} %param.19) | copy-start | bytes 147460
  22.5 5.7 %copy-start.8 = (s32[1,1,4096]{2,1,0:T(1,128)S(1)}, s32[1,1,4096]{2,1,0:T(1,128)}, u32[]{:S(2)}) copy-start(s32[1,1,4096]{2,1,0:T(1,128)} %param.18) | copy-start | bytes 49156
  28.2 22.2 %collective-permute-start.6 = (f32[1312,128]{1,0:T(8,128)S(1)}, f32[1312,128]{1,0:T(8,128)}, u32[]{:S(2)}, u32[]{:S(2)}) collective-permute-start(f32[1312,128]{1,0:T(8,128)S(1)} %get-tuple-element.155), channel_id=1, source_target_pairs={{16,20},{17,21},{18,22},{19,23},{20,24},{21,25},{22,26},{23,27},{2... | collective-permute-start | bytes 2015240 | tf_op jit(solution)/shard_map/cond/branch_3_fun/ppermute | solution.py:578
  38.7 11.6 %all-to-all-start.3 = ((f32[32,8,128]{2,1,0:T(8,128)}), f32[32,8,128]{2,1,0:T(8,128)}, u32[]{:S(2)}, u32[]{:S(2)}) async-start(f32[32,8,128]{2,1,0:T(8,128)} %get-tuple-element.154), calls=%async_computation.3 | async-start | bytes 262144 | tf_op jit(solution)/shard_map/cond/branch_3_fun/all_to_all | solution.py:540
  42.7 7.4 %collective-permute-start.7 = (f32[128,128]{1,0:T(8,128)}, f32[128,128]{1,0:T(8,128)}, u32[]{:S(2)}, u32[]{:S(2)}) collective-permute-start(f32[128,128]{1,0:T(8,128)} %get-tuple-element.281), channel_id=1, source_target_pairs={{16,20},{17,21},{18,22},{19,23},{20,24},{21,25},{22,26},{23,27},{2... | collective-permute-start | bytes 196616 | tf_op jit(solution)/shard_map/cond/branch_3_fun/ppermute | solution.py:578
where the time goes:
time: 55.1 us; the launch traced here: 54.7 us
  Pallas kernels  24.6 us (45%)
  starting transfers between devices  19.5 us (35%)
  waiting for transfers between devices  6.62 us (12%)
  local copies, waits for them, and re-layouts  2.91 us (5%)
  between operations  0.95 us (2%)
    pallas_call x1, Pallas kernels, relay(): pl.pallas_call(functools.partial(relay_kernel, tile=tile, nf=nf, edges=ed...  7.93 us
    all_to_all x2, starting transfers between devices, exchange(): return lax.all_to_all(values, ('mesh', 'blk'), 0, 0, tiled=True)  7.49 us
    pallas_call x1, Pallas kernels, interp(): pl.pallas_call(functools.partial(interp_kernel, tile=tile, blocks=blocks,...  6.81 us
    ppermute x2, starting transfers between devices, shift(): return lax.ppermute(v, ('mesh', 'blk'), pairs)  5.9 us
    ppermute x2, waiting for transfers between devices, shift(): return lax.ppermute(v, ('mesh', 'blk'), pairs)  4.13 us
    pallas_call x1, Pallas kernels, finish(): pl.pallas_call(functools.partial(finish_kernel, edges=len(e) == 2, blocks...  4.13 us
    ppermute x1, starting transfers between devices, local(): lax.ppermute(low, 'blk', [((i + 1) % blocks, i) for i in range(blocks)])  4.06 us
    pallas_call x1, Pallas kernels, march(): pl.pallas_call(march_kernel, out_shape=(jax.ShapeDtypeStruct((nf * npl, n...  3.41 us
  transfers between devices with their start and end apart: 6, of which 3 were waited for; matrix products, arithmetic and copies ran while one was open for 0% of the time, Pallas kernels for 33%

commit v1 on v0

--- a/solution.py
+++ b/solution.py
@@ -112,15 +112,13 @@
     return out
 
 
-def pack_kernel(f_any, kap_any, al_any, lo_ref, hi_ref, f_ref, kap_ref, al_ref, sems):
+def pack_kernel(f_any, kap_any, al_any, lo_any, hi_any, f_ref, kap_ref, al_ref, lo_ref, hi_ref, sems):
     nf, nz, npl = f_ref.shape
     copies = [pltpu.make_async_copy(f_any.at[f], f_ref.at[f], sems.at[f]) for f in range(nf)]
     copies += [pltpu.make_async_copy(kap_any.at[k], kap_ref.at[k], sems.at[nf + k]) for k in range(2)]
     copies += [pltpu.make_async_copy(al_any, al_ref, sems.at[nf + 2])]
     for c in copies:
         c.start()
-    for c in copies:
-        c.wait()
     lane = lanes(nz)
     per, nt = 128 // CY, npl // 128
 
@@ -131,10 +129,23 @@
         sl = slice(t*128, (t+1)*128)
         return kap_ref[f, :, sl] if f < 2 else al_ref[:, sl]
 
-    for ref, t, x, step in ((lo_ref, 0, 0, 1), (hi_ref, nt - 1, per - 1, -1)):
+    sides = ((lo_ref, lo_any, 0, 0, 1), (hi_ref, hi_any, nt - 1, per - 1, -1))
+    back = [pltpu.make_async_copy(ref.at[j], out.at[j], sems.at[nf + 3 + 3 * i + j])
+            for i, (ref, out, *_) in enumerate(sides) for j in range(3)]
+    for c in copies[:nf]:
+        c.wait()
+    for i, (ref, _, t, x, step) in enumerate(sides):
         ref[0] = pack_planes(field, nf, t, x, lane)
+        back[3 * i].start()
         ref[1] = pack_planes(field, nf, t, x + step, lane)
+        back[3 * i + 1].start()
+    for c in copies[nf:]:
+        c.wait()
+    for i, (ref, _, t, x, step) in enumerate(sides):
         ref[2] = pack_planes(coef, 3, t, x, lane)
+        back[3 * i + 2].start()
+    for c in back:
+        c.wait()
 
 
 def pack(fields, kappa, along):
@@ -144,8 +155,9 @@
         pack_kernel,
         out_shape=(sh, sh),
         in_specs=[ANY] * 3,
-        out_specs=(VM, VM),
-        scratch_shapes=[pltpu.VMEM(v.shape, F32) for v in (fields, kappa, along)] + [pltpu.SemaphoreType.DMA((nf + 3,))],
+        out_specs=(ANY, ANY),
+        scratch_shapes=[pltpu.VMEM(v.shape, F32) for v in (fields, kappa, along, sh, sh)]
+        + [pltpu.SemaphoreType.DMA((nf + 9,))],
         compiler_params=WHOLE,
         name="pack",
     )(fields, kappa, along)
@@ -437,11 +449,12 @@
     )(turn, arrived, cells, f1t, fac, base, frac)
 
 
-def finish_kernel(turn_ref, arr_ref, own_ref, moved_ref, e_ref, came_ref, *rest, edges, blocks, turned):
+def finish_kernel(turn_ref, arr_any, own_ref, moved_ref, e_any, came_any, *refs, edges, blocks, turned):
     if edges:
-        o_ref, pay_ref, ys, gs, *fac, sems = rest
+        out_any, *refs = refs
     else:
-        el_ref, er_ref, o_ref, pay_ref, ys, gs, *fac, sems = rest
+        el_ref, er_ref, out_any, *refs = refs
+    arr_ref, e_ref, o_ref, pay_ref, ys, gs, *fac, sems = refs
     nf, nz, npl = o_ref.shape
     nt = npl // 128
     nx = npl // CY
@@ -450,27 +463,37 @@
     j = nf * nt
     cells0 = (j + 2) * nz
     slots = (pay_ref.shape[0] - cells0) * 128
-    info_ref = places(turn_ref[0], arr_ref.shape[0] // 2, blocks, turned)
-
     lines = slice(j * nz, pay_ref.shape[0])
     rest = slice(0, j * nz)
-
-    def copies(ref):
-        return [pltpu.make_async_copy(ref.at[s], pay_ref.at[s], sems.at[i]) for i, s in enumerate((lines, rest))]
-
-    @pl.when(info_ref[3] == 0)
+    came = pltpu.make_async_copy(arr_any, arr_ref, sems.at[2])
+    came.start()
+
+    def copies(ref, e):
+        pairs = [(ref.at[s], pay_ref.at[s]) for s in (lines, rest)] + [(e, e_ref)]
+        return [pltpu.make_async_copy(a, b, sems.at[i]) for i, (a, b) in zip((0, 1, 3), pairs)]
+
+    back = lax.axis_index("mesh")
+
+    @pl.when(back == 0)
     def _():
-        for c in copies(own_ref):
+        for c in copies(own_ref, e_any):
             c.start()
 
-    @pl.when(info_ref[3] != 0)
+    @pl.when(back != 0)
     def _():
-        for c in copies(moved_ref):
+        for c in copies(moved_ref, came_any):
             c.start()
 
+    info_ref = places(turn_ref[0], arr_ref.shape[0] // 2, blocks, turned)
+    held = copies(own_ref, e_any)
     lane = lanes(nz)
     q = lane % nq
-    e = jnp.where(info_ref[3] == 0, e_ref[...], came_ref[...])
+    held[0].wait()
+    gs[...] = pay_ref[(j+1)*nz:(j+2)*nz, :]
+    factor(gs, *fac)
+    came.wait()
+    held[2].wait()
+    e = e_ref[...]
     if edges:
         chunks = arr_ref.shape[0] // 2
         el = arr_ref[chunks - info_ref[1] + lax.rem(info_ref[4] + chunks - 1, chunks)]
@@ -488,9 +511,6 @@
     left = jnp.where(q < 2, left, pltpu.roll(e, 2, axis=1))
     right = jnp.where(q >= nq - 2, right, pltpu.roll(e, 126, axis=1))
     deep = pltpu.roll(e, half, axis=1)
-    copies(own_ref)[0].wait()
-    gs[...] = pay_ref[(j+1)*nz:(j+2)*nz, :]
-    factor(gs, *fac)
 
     def cell_row(g, tile):
         per = tile // 128
@@ -509,13 +529,17 @@
     near = jnp.where(k % 128 < half, 1, 2)
     target = jnp.where(k < 128, spots(k, nf, npl, 0, CY - 1), spots(k, nf, npl, near, CY - 1 - near))
     fringe = on_fringe(lane)
-    copies(own_ref)[1].wait()
+    held[1].wait()
+    leave = [pltpu.make_async_copy(o_ref.at[f], out_any.at[f], sems.at[4 + f]) for f in range(nf)]
     for f in range(nf):
         put = (lax.broadcasted_iota(jnp.int32, (384, npl), 1) + f * npl == target).astype(F32).astype(BF)
         add = jnp.dot(terms, put, preferred_element_type=F32)
         for t in range(nt):
             v = pay_ref[(f*nt+t)*nz:(f*nt+t+1)*nz, :]
             o_ref[f, :, t*128:(t+1)*128] = jnp.where(fringe, 0.0, v) + add[:, t*128:(t+1)*128]
+        leave[f].start()
+    for c in leave:
+        c.wait()
 
 
 def finish(turn, shape, arrived, own, moved, e, blocks, turned):
@@ -523,10 +547,11 @@
     return pl.pallas_call(
         functools.partial(finish_kernel, edges=len(e) == 2, blocks=blocks, turned=turned),
         out_shape=jax.ShapeDtypeStruct(shape, F32),
-        in_specs=[SM, VM, ANY, ANY] + [VM] * len(e),
-        out_specs=VM,
-        scratch_shapes=[pltpu.VMEM(own.shape, F32)] + [pltpu.VMEM((nz, 128), F32)] * 9 + [pltpu.SemaphoreType.DMA((2,))],
-        compiler_params=CP,
+        in_specs=[SM] + [ANY] * 5 + [VM] * (len(e) - 2),
+        out_specs=ANY,
+        scratch_shapes=[pltpu.VMEM(v.shape, F32) for v in (arrived, e[0])] + [pltpu.VMEM(shape, F32), pltpu.VMEM(own.shape, F32)]
+        + [pltpu.VMEM((nz, 128), F32)] * 9 + [pltpu.SemaphoreType.DMA((4 + shape[0],))],
+        compiler_params=WHOLE,
         name="finish",
     )(turn, arrived, own, moved, *e)
 

time: 55.1 us -> 55.5 us (level); the launches traced: 54.7 us -> 55.7 us
  starting transfers between devices: 19.5 us -> 20.4 us
    all_to_all x2, waiting for transfers between devices: 2.48 us -> 1.53 us  [exchange(): return lax.all_to_all(values, ('mesh', 'blk'), 0, 0, tiled=True)]
    pallas_call x1, Pallas kernels: 4.13 us -> 3.36 us  [finish(): pl.pallas_call(functools.partial(finish_kernel, edges=len(e) == 2, blocks...]
    pallas_call x1, Pallas kernels: 3.41 us -> 4.16 us  [march(): pl.pallas_call(march_kernel, out_shape=(jax.ShapeDtypeStruct((nf * npl, n...]
    ppermute x2, waiting for transfers between devices: 4.13 us -> 4.82 us  [shift(): return lax.ppermute(v, ('mesh', 'blk'), pairs)]
    ppermute x2, starting transfers between devices: 5.9 us -> 6.57 us  [shift(): return lax.ppermute(v, ('mesh', 'blk'), pairs)]
  transfers between devices with their start and end apart: 6 -> 6, of which waited for: 3 -> 2; matrix products, arithmetic and copies ran while one was open for 0% -> 0% of each run, Pallas kernels for 33% -> 34%
where the time goes in v1:
time: 55.5 us; the launch traced here: 55.7 us
  Pallas kernels  24.5 us (44%)
  starting transfers between devices  20.4 us (37%)
  waiting for transfers between devices  6.35 us (11%)
  local copies, waits for them, and re-layouts  2.91 us (5%)
  between operations  0.95 us (2%)
    pallas_call x1, Pallas kernels, relay(): pl.pallas_call(functools.partial(relay_kernel, tile=tile, nf=nf, edges=ed...  7.94 us
    all_to_all x2, starting transfers between devices, exchange(): return lax.all_to_all(values, ('mesh', 'blk'), 0, 0, tiled=True)  7.7 us
    pallas_call x1, Pallas kernels, interp(): pl.pallas_call(functools.partial(interp_kernel, tile=tile, blocks=blocks,...  6.82 us
    ppermute x2, starting transfers between devices, shift(): return lax.ppermute(v, ('mesh', 'blk'), pairs)  6.57 us
    ppermute x2, waiting for transfers between devices, shift(): return lax.ppermute(v, ('mesh', 'blk'), pairs)  4.82 us
    pallas_call x1, Pallas kernels, march(): pl.pallas_call(march_kernel, out_shape=(jax.ShapeDtypeStruct((nf * npl, n...  4.16 us
    ppermute x1, starting transfers between devices, local(): lax.ppermute(low, 'blk', [((i + 1) % blocks, i) for i in range(blocks)])  4.06 us
    pallas_call x1, Pallas kernels, finish(): pl.pallas_call(functools.partial(finish_kernel, edges=len(e) == 2, blocks...  3.36 us
  transfers between devices with their start and end apart: 6, of which 2 were waited for; matrix products, arithmetic and copies ran while one was open for 0% of the time, Pallas kernels for 34%

profile of v1, /device:TPU:1, one launch (start us, length us, event | category | flops | bytes accessed | tf_op | source)
XLA Modules:
  0.0 55.7 jit_solution(12408693268272140784)
XLA Ops:
  0.0 2.3 %pack.1 = (f32[3,128,128]{2,1,0:T(8,128)}, f32[3,128,128]{2,1,0:T(8,128)}) custom-call(f32[4,128,256]{2,1,0:T(8,128)} %bitcast.43, f32[2,128,256]{2,1,0:T(8,128)} %bitcast.46, f32[128,256]{1,0:T(8,128)} %bitcast.48), custom_call_target="tpu_custom_call" | custom-call | tf_op jit(solution)/shard_map/pack/pallas_call | solution.py:154
  2.3 2.1 %collective-permute-start.14 = (f32[3,128,128]{2,1,0:T(8,128)}, f32[3,128,128]{2,1,0:T(8,128)S(1)}, u32[]{:S(2)}, u32[]{:S(2)}) collective-permute-start(f32[3,128,128]{2,1,0:T(8,128)} %get-tuple-element.199.hi_ref), channel_id=1, source_target_pairs={{0,1},{1,2},{2,3},{3,4},{4,5},{5,6},{6,7},{7,8},{8,9},{9,10},{10,1... | collective-permute-start | bytes 589832 | tf_op jit(solution)/shard_map/ppermute | solution.py:595
  4.4 4.1 %collective-permute-start.15 = (f32[3,128,128]{2,1,0:T(8,128)}, f32[3,128,128]{2,1,0:T(8,128)S(1)}, u32[]{:S(2)}, u32[]{:S(2)}) collective-permute-start(f32[3,128,128]{2,1,0:T(8,128)} %get-tuple-element.200.lo_ref), channel_id=1, source_target_pairs={{1,0},{2,1},{3,2},{4,3},{5,4},{6,5},{7,6},{8,7},{9,8},{10,9},{11,1... | collective-permute-start | bytes 589832 | tf_op jit(solution)/shard_map/ppermute | solution.py:596
  9.1 0.0 copy-start
  9.1 1.0 %copy-done = f32[1,1,4,128,256]{4,3,2,1,0:T(8,128)S(1)} copy-done((f32[1,1,4,128,256]{4,3,2,1,0:T(8,128)S(1)}, f32[1,1,4,128,256]{4,3,2,1,0:T(8,128)}, u32[]{:S(2)}) %copy-start) | copy-done | bytes 524312
  10.1 0.0 copy-start.1
  10.1 0.0 copy-start.3
  10.1 0.0 copy-start.7
  10.1 6.8 %interp.1 = f32[32,8,128]{2,1,0:T(8,128)} custom-call(s32[1]{0:T(128)S(6)} %copy.43.turn_any.turn_ref, f32[4,128,256]{2,1,0:T(8,128)S(1)} %bitcast.44, s32[1,4096]{1,0:T(1,128)} %bitcast.66, f32[3,1,4096]{2,1,0:T(1,128)} %bitcast.50), custom_call_target="tpu_custom_call" | custom-call | tf_op jit(solution)/shard_map/interp/pallas_call | solution.py:233
  17.0 0.0 copy-start.2
  17.0 0.0 collective-permute-done.14.left_ref
  17.0 0.0 collective-permute-done.15.right_ref
  17.0 3.5 %all-to-all-start.7 = ((f32[32,8,128]{2,1,0:T(8,128)}), f32[32,8,128]{2,1,0:T(8,128)S(1)}, u32[]{:S(2)}, u32[]{:S(2)}) async-start(f32[32,8,128]{2,1,0:T(8,128)} %interp.1), calls=%async_computation.7 | async-start | bytes 262144 | tf_op jit(solution)/shard_map/all_to_all | solution.py:565
  20.5 0.0 copy-done.1
  20.5 0.0 copy-done.3
  20.5 0.0 copy-done.7
  20.5 0.0 copy-done.2
  20.5 0.0 copy-start.4
  20.6 0.9 %copy-done.4 = f32[3,128,128]{2,1,0:T(8,128)S(1)} copy-done((f32[3,128,128]{2,1,0:T(8,128)S(1)}, f32[3,128,128]{2,1,0:T(8,128)}, u32[]{:S(2)}) %copy-start.4) | copy-done | bytes 196632
  21.5 0.0 copy-start.5
  21.5 0.9 %copy-done.5 = f32[3,128,128]{2,1,0:T(8,128)S(1)} copy-done((f32[3,128,128]{2,1,0:T(8,128)S(1)}, f32[3,128,128]{2,1,0:T(8,128)}, u32[]{:S(2)}) %copy-start.5) | copy-done | bytes 196632
  22.4 0.0 copy-start.6
  22.4 0.0 copy-start.8
  22.4 4.2 %march.1 = (f32[1024,128]{1,0:T(8,128)S(1)}, f32[1312,128]{1,0:T(8,128)}, f32[1024,128]{1,0:T(8,128)S(1)}) custom-call(f32[4,128,256]{2,1,0:T(8,128)S(1)} %bitcast.45, f32[2,128,256]{2,1,0:T(8,128)S(1)} %bitcast.47, f32[128,256]{1,0:T(8,128)S(1)} %bitcast.49, f32[3,128,128]{2,1,0:T(8,128)S(1)} %copy-done.4, f32[3,128,128]{2,1,0:T(8,128)S(1)} %copy-done.5, ...), custom_call_target="tpu_custom_call" | custom-call | tf_op jit(solution)/shard_map/march/pallas_call | solution.py:356
  26.6 1.5 %all-to-all-done.7 = f32[32,8,128]{2,1,0:T(8,128)S(1)} async-done(((f32[32,8,128]{2,1,0:T(8,128)}), f32[32,8,128]{2,1,0:T(8,128)S(1)}, u32[]{:S(2)}, u32[]{:S(2)}) %all-to-all-start.7) | async-done | bytes 131104 | tf_op jit(solution)/shard_map/all_to_all | solution.py:565
  28.1 0.0 copy-done.6
  28.1 0.0 copy-done.8
  28.1 24.0 %conditional.1 = (f32[32,8,128]{2,1,0:T(8,128)}, f32[1312,128]{1,0:T(8,128)}, f32[128,128]{1,0:T(8,128)}, f32[128,128]{1,0:T(8,128)}) conditional(s32[]{:T(128)} %bitcast.35, (s32[1,1,4096]{2,1,0:T(1,128)S(1)}, s32[1,1,4096]{2,1,0:T(1,128)S(1)}, f32[1,1,3,4096]{3,1,2,0:T(1,128)S(1)}, s32[1]{0:T(128)}, ...), branch_computations={%region_0.0_spmd, %region_1.0_spmd, %region_2.0_spmd, %region_3.0_... | conditional | bytes 3342480 | solution.py:620
  28.1 3.3 %collective-permute-start.2 = (f32[1312,128]{1,0:T(8,128)}, f32[1312,128]{1,0:T(8,128)}, u32[]{:S(2)}, u32[]{:S(2)}) collective-permute-start(f32[1312,128]{1,0:T(8,128)} %get-tuple-element.135), channel_id=1, source_target_pairs={{16,18},{17,19},{18,20},{19,21},{20,22},{21,23},{22,24},{23,25},{2... | collective-permute-start | bytes 2015240 | tf_op jit(solution)/shard_map/cond/branch_1_fun/ppermute | solution.py:603
  31.4 7.9 %relay.8 = (f32[32,8,128]{2,1,0:T(8,128)}, f32[128,128]{1,0:T(8,128)}) custom-call(s32[1]{0:T(128)} %get-tuple-element.127.turn_ref, f32[32,8,128]{2,1,0:T(8,128)S(1)} %get-tuple-element.128.arr_ref, s32[1,4096]{1,0:T(1,128)S(1)} %bitcast.60, f32[1024,128]{1,0:T(8,128)S(1)} %get-tuple-element.130.f1t_ref, f32[1024,128]{1,0:T(8,128)S(1)} %get-tuple-element.131.fac_ref, ...), custom_call_target="tpu_custom_call" | custom-call | tf_op jit(solution)/shard_map/cond/branch_1_fun/relay/pallas_call | solution.py:441
  39.3 4.2 %all-to-all-start.1 = ((f32[32,8,128]{2,1,0:T(8,128)}), f32[32,8,128]{2,1,0:T(8,128)}, u32[]{:S(2)}, u32[]{:S(2)}) async-start(f32[32,8,128]{2,1,0:T(8,128)} %get-tuple-element.134), calls=%async_computation.1 | async-start | bytes 262144 | tf_op jit(solution)/shard_map/cond/branch_1_fun/all_to_all | solution.py:565
  43.5 3.3 %collective-permute-start.3 = (f32[128,128]{1,0:T(8,128)}, f32[128,128]{1,0:T(8,128)}, u32[]{:S(2)}, u32[]{:S(2)}) collective-permute-start(f32[128,128]{1,0:T(8,128)} %get-tuple-element.273), channel_id=1, source_target_pairs={{16,18},{17,19},{18,20},{19,21},{20,22},{21,23},{22,24},{23,25},{2... | collective-permute-start | bytes 196616 | tf_op jit(solution)/shard_map/cond/branch_1_fun/ppermute | solution.py:603
  46.8 4.8 %collective-permute-done.3 = f32[128,128]{1,0:T(8,128)} collective-permute-done((f32[128,128]{1,0:T(8,128)}, f32[128,128]{1,0:T(8,128)}, u32[]{:S(2)}, u32[]{:S(2)}) %collective-permute-start.3) | collective-permute-done | bytes 65568 | tf_op jit(solution)/shard_map/cond/branch_1_fun/ppermute | solution.py:603
  51.6 0.0 all-to-all-done.1
  51.6 0.0 collective-permute-done.2
  52.1 3.4 %finish.1 = f32[4,128,256]{2,1,0:T(8,128)} custom-call(s32[1]{0:T(128)S(6)} %copy.43.turn_any.turn_ref, f32[32,8,128]{2,1,0:T(8,128)} %get-tuple-element.207.arr_any, f32[1312,128]{1,0:T(8,128)} %get-tuple-element.206.own_ref, f32[1312,128]{1,0:T(8,128)} %get-tuple-element.208.moved_ref, f32[128,128]{1,0:T(8,128)} %get-tuple-element.209.e_any, ...), custom_call_target="tpu_custom_call" | custom-call | tf_op jit(solution)/shard_map/finish/pallas_call | solution.py:547
Async XLA Ops:
  2.3 14.7 %collective-permute-start.14 = (f32[3,128,128]{2,1,0:T(8,128)}, f32[3,128,128]{2,1,0:T(8,128)S(1)}, u32[]{:S(2)}, u32[]{:S(2)}) collective-permute-start(f32[3,128,128]{2,1,0:T(8,128)} %get-tuple-element.199.hi_ref), channel_id=1, source_target_pairs={{0,1},{1,2},{2,3},{3,4},{4,5},{5,6},{6,7},{7,8},{8,9},{9,10},{10,1... | collective-permute-start | bytes 589832 | tf_op jit(solution)/shard_map/ppermute | solution.py:595
  4.4 12.6 %collective-permute-start.15 = (f32[3,128,128]{2,1,0:T(8,128)}, f32[3,128,128]{2,1,0:T(8,128)S(1)}, u32[]{:S(2)}, u32[]{:S(2)}) collective-permute-start(f32[3,128,128]{2,1,0:T(8,128)} %get-tuple-element.200.lo_ref), channel_id=1, source_target_pairs={{1,0},{2,1},{3,2},{4,3},{5,4},{6,5},{7,6},{8,7},{9,8},{10,9},{11,1... | collective-permute-start | bytes 589832 | tf_op jit(solution)/shard_map/ppermute | solution.py:596
  9.1 1.0 %copy-start = (f32[1,1,4,128,256]{4,3,2,1,0:T(8,128)S(1)}, f32[1,1,4,128,256]{4,3,2,1,0:T(8,128)}, u32[]{:S(2)}) copy-start(f32[1,1,4,128,256]{4,3,2,1,0:T(8,128)} %param.15) | copy-start | bytes 1572868
  10.1 10.4 %copy-start.1 = (f32[1,1,4,128,256]{4,3,2,1,0:T(8,128)S(1)}, f32[1,1,4,128,256]{4,3,2,1,0:T(8,128)}, u32[]{:S(2)}) copy-start(f32[1,1,4,128,256]{4,3,2,1,0:T(8,128)} %param.15) | copy-start | bytes 1572868
  10.1 10.4 %copy-start.3 = (f32[1,1,128,256]{3,2,1,0:T(8,128)S(1)}, f32[1,1,128,256]{3,2,1,0:T(8,128)}, u32[]{:S(2)}) copy-start(f32[1,1,128,256]{3,2,1,0:T(8,128)} %param.17) | copy-start | bytes 393220
  10.1 10.4 %copy-start.7 = (s32[1,1,4096]{2,1,0:T(1,128)S(1)}, s32[1,1,4096]{2,1,0:T(1,128)}, u32[]{:S(2)}) copy-start(s32[1,1,4096]{2,1,0:T(1,128)} %param.20) | copy-start | bytes 49156
  17.0 3.6 %copy-start.2 = (f32[1,1,2,128,256]{4,3,2,1,0:T(8,128)S(1)}, f32[1,1,2,128,256]{4,3,2,1,0:T(8,128)}, u32[]{:S(2)}) copy-start(f32[1,1,2,128,256]{4,3,2,1,0:T(8,128)} %param.16) | copy-start | bytes 786436
  17.0 11.1 %all-to-all-start.7 = ((f32[32,8,128]{2,1,0:T(8,128)}), f32[32,8,128]{2,1,0:T(8,128)S(1)}, u32[]{:S(2)}, u32[]{:S(2)}) async-start(f32[32,8,128]{2,1,0:T(8,128)} %interp.1), calls=%async_computation.7 | async-start | bytes 262144 | tf_op jit(solution)/shard_map/all_to_all | solution.py:565
  20.5 0.9 %copy-start.4 = (f32[3,128,128]{2,1,0:T(8,128)S(1)}, f32[3,128,128]{2,1,0:T(8,128)}, u32[]{:S(2)}) copy-start(f32[3,128,128]{2,1,0:T(8,128)} %get-tuple-element.200.lo_ref) | copy-start | bytes 589828
  21.5 0.9 %copy-start.5 = (f32[3,128,128]{2,1,0:T(8,128)S(1)}, f32[3,128,128]{2,1,0:T(8,128)}, u32[]{:S(2)}) copy-start(f32[3,128,128]{2,1,0:T(8,128)} %get-tuple-element.199.hi_ref) | copy-start | bytes 589828
  22.4 5.7 %copy-start.6 = (f32[1,1,3,4096]{3,1,2,0:T(1,128)S(1)}, f32[1,1,3,4096]{3,1,2,0:T(1,128)}, u32[]{:S(2)}) copy-start(f32[1,1,3,4096]{3,1,2,0:T(1,128)} %param.19) | copy-start | bytes 147460
  22.4 5.7 %copy-start.8 = (s32[1,1,4096]{2,1,0:T(1,128)S(1)}, s32[1,1,4096]{2,1,0:T(1,128)}, u32[]{:S(2)}) copy-start(s32[1,1,4096]{2,1,0:T(1,128)} %param.18) | copy-start | bytes 49156
  28.1 23.6 %collective-permute-start.2 = (f32[1312,128]{1,0:T(8,128)}, f32[1312,128]{1,0:T(8,128)}, u32[]{:S(2)}, u32[]{:S(2)}) collective-permute-start(f32[1312,128]{1,0:T(8,128)} %get-tuple-element.135), channel_id=1, source_target_pairs={{16,18},{17,19},{18,20},{19,21},{20,22},{21,23},{22,24},{23,25},{2... | collective-permute-start | bytes 2015240 | tf_op jit(solution)/shard_map/cond/branch_1_fun/ppermute | solution.py:603
  39.3 12.3 %all-to-all-start.1 = ((f32[32,8,128]{2,1,0:T(8,128)}), f32[32,8,128]{2,1,0:T(8,128)}, u32[]{:S(2)}, u32[]{:S(2)}) async-start(f32[32,8,128]{2,1,0:T(8,128)} %get-tuple-element.134), calls=%async_computation.1 | async-start | bytes 262144 | tf_op jit(solution)/shard_map/cond/branch_1_fun/all_to_all | solution.py:565
  43.5 8.1 %collective-permute-start.3 = (f32[128,128]{1,0:T(8,128)}, f32[128,128]{1,0:T(8,128)}, u32[]{:S(2)}, u32[]{:S(2)}) collective-permute-start(f32[128,128]{1,0:T(8,128)} %get-tuple-element.273), channel_id=1, source_target_pairs={{16,18},{17,19},{18,20},{19,21},{20,22},{21,23},{22,24},{23,25},{2... | collective-permute-start | bytes 196616 | tf_op jit(solution)/shard_map/cond/branch_1_fun/ppermute | solution.py:603

commit v2 on v1

--- a/solution.py
+++ b/solution.py
@@ -339,9 +339,10 @@
     cs = c * inv
     gg = 2.0 + (inv + 4.0 * cs)
     j = nf * nt
-    pay_ref[j*nz:(j+1)*nz, :] = cs
-    pay_ref[(j+1)*nz:(j+2)*nz, :] = gg
-    pay_ref[(j+2)*nz:, :] = cells_ref[...].astype(F32)
+    few = (lane // (4 * nx) % 2) * (nf - 1) * 2 * nx + (lane // (2 * nx) % 2) * half + ln % (2 * nx)
+    pay_ref[j*nz:(j+1)*nz, :] = jnp.where(
+        lane < half, jnp.take_along_axis(cs, few, axis=1), jnp.take_along_axis(gg, few, axis=1))
+    pay_ref[(j+1)*nz:, :] = cells_ref[...].astype(F32)
     gs[...] = gg
     refs = [fac_ref.at[i*nz:(i+1)*nz] for i in range(7)]
     factor(gs, *refs)
@@ -351,7 +352,7 @@
 def march(start, kappa, along, low, high, left, right, cells):
     nf, nz, npl = start.shape
     nt = npl // 128
-    rows = (nf * nt + 2) * nz + cells.shape[0]
+    rows = (nf * nt + 1) * nz + cells.shape[0]
     w = 2 * npl + 256
     return pl.pallas_call(
         march_kernel,
@@ -415,7 +416,8 @@
     ys[...] = reduce_rhs(fac[7][...] * fr, slice(0, 128), fac[:5])
     substitute(ys, fac[5], fac[6], same)
     e = ys[...]
-    e_ref[...] = e
+    low = lax.broadcasted_iota(jnp.int32, (nz // 2, 128), 1) < half
+    e_ref[...] = jnp.where(low, e[:nz//2], pltpu.roll(e[nz//2:], half, axis=1))
     hi, lo = split2(e)
     both = jnp.where(lane < half, hi.astype(F32), pltpu.roll(lo.astype(F32), half, axis=1))
     terms = jnp.concatenate([sm.astype(BF), both.astype(BF)], axis=1)
@@ -440,13 +442,17 @@
     nz = f1t.shape[1]
     return pl.pallas_call(
         functools.partial(relay_kernel, tile=tile, nf=nf, edges=edges, blocks=blocks, turned=turned),
-        out_shape=(jax.ShapeDtypeStruct(arrived.shape, F32), jax.ShapeDtypeStruct((nz, 128), F32)),
+        out_shape=(jax.ShapeDtypeStruct(arrived.shape, F32), jax.ShapeDtypeStruct((nz // 2, 128), F32)),
         in_specs=[SM] + [VM] * 6,
         out_specs=(VM, VM),
         scratch_shapes=[pltpu.VMEM((f1t.shape[0], 4 * nz), BF), pltpu.VMEM((nz, 128), F32)],
         compiler_params=CP,
         name="relay",
     )(turn, arrived, cells, f1t, fac, base, frac)
+
+
+def unfold(v):
+    return jnp.concatenate([v, pltpu.roll(v, 64, axis=1)], axis=0)
 
 
 def finish_kernel(turn_ref, arr_any, own_ref, moved_ref, e_any, came_any, *refs, edges, blocks, turned):
@@ -461,7 +467,7 @@
     nq = 2 * nx
     half = nf * nq
     j = nf * nt
-    cells0 = (j + 2) * nz
+    cells0 = (j + 1) * nz
     slots = (pay_ref.shape[0] - cells0) * 128
     lines = slice(j * nz, pay_ref.shape[0])
     rest = slice(0, j * nz)
@@ -489,11 +495,15 @@
     lane = lanes(nz)
     q = lane % nq
     held[0].wait()
-    gs[...] = pay_ref[(j+1)*nz:(j+2)*nz, :]
+    ln = lane % half
+    few = ln // nq // (nf - 1) * 2 * nq + lane // half * nq + ln % nq
+    table = pay_ref[j*nz:(j+1)*nz, :]
+    cs = jnp.take_along_axis(table, few, axis=1)
+    gs[...] = jnp.take_along_axis(table, few + half, axis=1)
     factor(gs, *fac)
     came.wait()
     held[2].wait()
-    e = e_ref[...]
+    e = unfold(e_ref[...])
     if edges:
         chunks = arr_ref.shape[0] // 2
         el = arr_ref[chunks - info_ref[1] + lax.rem(info_ref[4] + chunks - 1, chunks)]
@@ -506,8 +516,8 @@
         outer = jnp.concatenate([parts, parts], axis=0).T
         left = right = outer
     else:
-        left = pltpu.roll(el_ref[...], 128 - (nq - 2), axis=1)
-        right = pltpu.roll(er_ref[...], nq - 2, axis=1)
+        left = pltpu.roll(unfold(el_ref[...]), 128 - (nq - 2), axis=1)
+        right = pltpu.roll(unfold(er_ref[...]), nq - 2, axis=1)
     left = jnp.where(q < 2, left, pltpu.roll(e, 2, axis=1))
     right = jnp.where(q >= nq - 2, right, pltpu.roll(e, 126, axis=1))
     deep = pltpu.roll(e, half, axis=1)
@@ -519,7 +529,6 @@
 
     sm = place_small(info_ref[0], arr_ref, info_ref[1], cell_row, slots, nf, nz, npl)
     fr = sm + pltpu.roll(sm, half, axis=1)
-    cs = pay_ref[j*nz:(j+1)*nz, :]
     r = cs * jnp.where(lane < half, fr + left + right, deep)
     ys[...] = reduce_rhs(r, slice(0, 128), fac[:5])
     substitute(ys, fac[5], fac[6], same)
@@ -551,7 +560,7 @@
         out_specs=ANY,
         scratch_shapes=[pltpu.VMEM(v.shape, F32) for v in (arrived, e[0])] + [pltpu.VMEM(shape, F32), pltpu.VMEM(own.shape, F32)]
         + [pltpu.VMEM((nz, 128), F32)] * 9 + [pltpu.SemaphoreType.DMA((4 + shape[0],))],
-        compiler_params=WHOLE,
+        compiler_params=CP,
         name="finish",
     )(turn, arrived, own, moved, *e)
 

time: 55.5 us -> 54.8 us (0.987); the launches traced: 55.7 us -> 54.4 us
  waiting for transfers between devices: 6.35 us -> 5.33 us
  starting transfers between devices: 20.4 us -> 21.3 us
  Pallas kernels: 24.5 us -> 23.8 us
    ppermute x2, waiting for transfers between devices: 4.82 us -> 3.08 us  [shift(): return lax.ppermute(v, ('mesh', 'blk'), pairs)]
    ppermute x2, starting transfers between devices: 6.57 us -> 8.25 us  [shift(): return lax.ppermute(v, ('mesh', 'blk'), pairs)]
    all_to_all x2, starting transfers between devices: 7.7 us -> 6.94 us  [exchange(): return lax.all_to_all(values, ('mesh', 'blk'), 0, 0, tiled=True)]
    pallas_call x1, Pallas kernels: 4.16 us -> 3.44 us  [march(): pl.pallas_call(march_kernel, out_shape=(jax.ShapeDtypeStruct((nf * npl, n...]
    all_to_all x2, waiting for transfers between devices: 1.53 us -> 2.25 us  [exchange(): return lax.all_to_all(values, ('mesh', 'blk'), 0, 0, tiled=True)]
  transfers between devices with their start and end apart: 6 -> 6, of which waited for: 2 -> 2; matrix products, arithmetic and copies ran while one was open for 0% -> 0% of each run, Pallas kernels for 34% -> 33%
where the time goes in v2:
time: 54.8 us; the launch traced here: 54.4 us
  Pallas kernels  23.8 us (43%)
  starting transfers between devices  21.3 us (39%)
  waiting for transfers between devices  5.33 us (10%)
  local copies, waits for them, and re-layouts  2.91 us (5%)
  between operations  0.95 us (2%)
    ppermute x2, starting transfers between devices, shift(): return lax.ppermute(v, ('mesh', 'blk'), pairs)  8.25 us
    pallas_call x1, Pallas kernels, relay(): pl.pallas_call(functools.partial(relay_kernel, tile=tile, nf=nf, edges=ed...  7.92 us
    all_to_all x2, starting transfers between devices, exchange(): return lax.all_to_all(values, ('mesh', 'blk'), 0, 0, tiled=True)  6.94 us
    pallas_call x1, Pallas kernels, interp(): pl.pallas_call(functools.partial(interp_kernel, tile=tile, blocks=blocks,...  6.81 us
    ppermute x1, starting transfers between devices, local(): lax.ppermute(low, 'blk', [((i + 1) % blocks, i) for i in range(blocks)])  4.06 us
    pallas_call x1, Pallas kernels, march(): pl.pallas_call(march_kernel, out_shape=(jax.ShapeDtypeStruct((nf * npl, n...  3.44 us
    pallas_call x1, Pallas kernels, finish(): pl.pallas_call(functools.partial(finish_kernel, edges=len(e) == 2, blocks...  3.39 us
    ppermute x2, waiting for transfers between devices, shift(): return lax.ppermute(v, ('mesh', 'blk'), pairs)  3.08 us
  transfers between devices with their start and end apart: 6, of which 2 were waited for; matrix products, arithmetic and copies ran while one was open for 0% of the time, Pallas kernels for 33%

profile of v2, /device:TPU:1, one launch (start us, length us, event | category | flops | bytes accessed | tf_op | source)
XLA Modules:
  0.0 54.4 jit_solution(13271896244124742990)
XLA Ops:
  0.0 2.3 %pack.1 = (f32[3,128,128]{2,1,0:T(8,128)}, f32[3,128,128]{2,1,0:T(8,128)}) custom-call(f32[4,128,256]{2,1,0:T(8,128)} %bitcast.43, f32[2,128,256]{2,1,0:T(8,128)} %bitcast.46, f32[128,256]{1,0:T(8,128)} %bitcast.48), custom_call_target="tpu_custom_call" | custom-call | tf_op jit(solution)/shard_map/pack/pallas_call | solution.py:154
  2.3 2.1 %collective-permute-start.14 = (f32[3,128,128]{2,1,0:T(8,128)}, f32[3,128,128]{2,1,0:T(8,128)S(1)}, u32[]{:S(2)}, u32[]{:S(2)}) collective-permute-start(f32[3,128,128]{2,1,0:T(8,128)} %get-tuple-element.199.hi_ref), channel_id=1, source_target_pairs={{0,1},{1,2},{2,3},{3,4},{4,5},{5,6},{6,7},{7,8},{8,9},{9,10},{10,1... | collective-permute-start | bytes 589832 | tf_op jit(solution)/shard_map/ppermute | solution.py:604
  4.4 4.1 %collective-permute-start.15 = (f32[3,128,128]{2,1,0:T(8,128)}, f32[3,128,128]{2,1,0:T(8,128)S(1)}, u32[]{:S(2)}, u32[]{:S(2)}) collective-permute-start(f32[3,128,128]{2,1,0:T(8,128)} %get-tuple-element.200.lo_ref), channel_id=1, source_target_pairs={{1,0},{2,1},{3,2},{4,3},{5,4},{6,5},{7,6},{8,7},{9,8},{10,9},{11,1... | collective-permute-start | bytes 589832 | tf_op jit(solution)/shard_map/ppermute | solution.py:605
  9.1 0.0 copy-start
  9.1 1.0 %copy-done = f32[1,1,4,128,256]{4,3,2,1,0:T(8,128)S(1)} copy-done((f32[1,1,4,128,256]{4,3,2,1,0:T(8,128)S(1)}, f32[1,1,4,128,256]{4,3,2,1,0:T(8,128)}, u32[]{:S(2)}) %copy-start) | copy-done | bytes 524312
  10.1 0.0 copy-start.1
  10.1 0.0 copy-start.3
  10.1 0.0 copy-start.7
  10.1 6.8 %interp.1 = f32[32,8,128]{2,1,0:T(8,128)} custom-call(s32[1]{0:T(128)S(6)} %copy.43.turn_any.turn_ref, f32[4,128,256]{2,1,0:T(8,128)S(1)} %bitcast.44, s32[1,4096]{1,0:T(1,128)} %bitcast.66, f32[3,1,4096]{2,1,0:T(1,128)} %bitcast.50), custom_call_target="tpu_custom_call" | custom-call | tf_op jit(solution)/shard_map/interp/pallas_call | solution.py:233
  16.9 0.0 copy-start.2
  17.0 0.0 collective-permute-done.14.left_ref
  17.0 0.0 collective-permute-done.15.right_ref
  17.0 3.5 %all-to-all-start.7 = ((f32[32,8,128]{2,1,0:T(8,128)}), f32[32,8,128]{2,1,0:T(8,128)S(1)}, u32[]{:S(2)}, u32[]{:S(2)}) async-start(f32[32,8,128]{2,1,0:T(8,128)} %interp.1), calls=%async_computation.7 | async-start | bytes 262144 | tf_op jit(solution)/shard_map/all_to_all | solution.py:574
  20.5 0.0 copy-done.1
  20.5 0.0 copy-done.3
  20.5 0.0 copy-done.7
  20.5 0.0 copy-done.2
  20.5 0.0 copy-start.4
  20.6 0.9 %copy-done.4 = f32[3,128,128]{2,1,0:T(8,128)S(1)} copy-done((f32[3,128,128]{2,1,0:T(8,128)S(1)}, f32[3,128,128]{2,1,0:T(8,128)}, u32[]{:S(2)}) %copy-start.4) | copy-done | bytes 196632
  21.5 0.0 copy-start.5
  21.5 0.9 %copy-done.5 = f32[3,128,128]{2,1,0:T(8,128)S(1)} copy-done((f32[3,128,128]{2,1,0:T(8,128)S(1)}, f32[3,128,128]{2,1,0:T(8,128)}, u32[]{:S(2)}) %copy-start.5) | copy-done | bytes 196632
  22.4 0.0 copy-start.6
  22.4 0.0 copy-start.8
  22.4 3.4 %march.1 = (f32[1024,128]{1,0:T(8,128)S(1)}, f32[1184,128]{1,0:T(8,128)S(1)}, f32[1024,128]{1,0:T(8,128)S(1)}) custom-call(f32[4,128,256]{2,1,0:T(8,128)S(1)} %bitcast.45, f32[2,128,256]{2,1,0:T(8,128)S(1)} %bitcast.47, f32[128,256]{1,0:T(8,128)S(1)} %bitcast.49, f32[3,128,128]{2,1,0:T(8,128)S(1)} %copy-done.4, f32[3,128,128]{2,1,0:T(8,128)S(1)} %copy-done.5, ...), custom_call_target="tpu_custom_call" | custom-call | tf_op jit(solution)/shard_map/march/pallas_call | solution.py:357
  25.8 2.2 %all-to-all-done.7 = f32[32,8,128]{2,1,0:T(8,128)S(1)} async-done(((f32[32,8,128]{2,1,0:T(8,128)}), f32[32,8,128]{2,1,0:T(8,128)S(1)}, u32[]{:S(2)}, u32[]{:S(2)}) %all-to-all-start.7) | async-done | bytes 131104 | tf_op jit(solution)/shard_map/all_to_all | solution.py:574
  28.1 0.0 copy-done.6
  28.1 0.0 copy-done.8
  28.1 22.7 %conditional.1 = (f32[32,8,128]{2,1,0:T(8,128)}, f32[1184,128]{1,0:T(8,128)}, f32[64,128]{1,0:T(8,128)}, f32[64,128]{1,0:T(8,128)}) conditional(s32[]{:T(128)} %bitcast.35, (s32[1,1,4096]{2,1,0:T(1,128)S(1)}, s32[1,1,4096]{2,1,0:T(1,128)S(1)}, f32[1,1,3,4096]{3,1,2,0:T(1,128)S(1)}, s32[1]{0:T(128)}, ...), branch_computations={%region_0.0_spmd, %region_1.0_spmd, %region_2.0_spmd, %region_3.0_... | conditional | bytes 2949264 | solution.py:629
  28.1 3.1 %collective-permute-start.12 = (f32[1184,128]{1,0:T(8,128)S(1)}, f32[1184,128]{1,0:T(8,128)}, u32[]{:S(2)}, u32[]{:S(2)}) collective-permute-start(f32[1184,128]{1,0:T(8,128)S(1)} %get-tuple-element.185), channel_id=1, source_target_pairs={{16,23},{17,24},{18,25},{19,26},{20,27},{21,28},{22,29},{23,30},{2... | collective-permute-start | bytes 1818632 | tf_op jit(solution)/shard_map/cond/branch_6_fun/ppermute | solution.py:612
  31.3 7.9 %relay.13 = (f32[32,8,128]{2,1,0:T(8,128)}, f32[64,128]{1,0:T(8,128)}) custom-call(s32[1]{0:T(128)} %get-tuple-element.177.turn_ref, f32[32,8,128]{2,1,0:T(8,128)S(1)} %get-tuple-element.178.arr_ref, s32[1,4096]{1,0:T(1,128)S(1)} %bitcast.65, f32[1024,128]{1,0:T(8,128)S(1)} %get-tuple-element.180.f1t_ref, f32[1024,128]{1,0:T(8,128)S(1)} %get-tuple-element.181.fac_ref, ...), custom_call_target="tpu_custom_call" | custom-call | tf_op jit(solution)/shard_map/cond/branch_6_fun/relay/pallas_call | solution.py:443
  39.2 3.4 %all-to-all-start.6 = ((f32[32,8,128]{2,1,0:T(8,128)}), f32[32,8,128]{2,1,0:T(8,128)}, u32[]{:S(2)}, u32[]{:S(2)}) async-start(f32[32,8,128]{2,1,0:T(8,128)} %get-tuple-element.184), calls=%async_computation.6 | async-start | bytes 262144 | tf_op jit(solution)/shard_map/cond/branch_6_fun/all_to_all | solution.py:574
  42.6 5.1 %collective-permute-start.13 = (f32[64,128]{1,0:T(8,128)}, f32[64,128]{1,0:T(8,128)}, u32[]{:S(2)}, u32[]{:S(2)}) collective-permute-start(f32[64,128]{1,0:T(8,128)} %get-tuple-element.293), channel_id=1, source_target_pairs={{16,23},{17,24},{18,25},{19,26},{20,27},{21,28},{22,29},{23,30},{2... | collective-permute-start | bytes 98312 | tf_op jit(solution)/shard_map/cond/branch_6_fun/ppermute | solution.py:612
  47.7 3.1 %collective-permute-done.13 = f32[64,128]{1,0:T(8,128)} collective-permute-done((f32[64,128]{1,0:T(8,128)}, f32[64,128]{1,0:T(8,128)}, u32[]{:S(2)}, u32[]{:S(2)}) %collective-permute-start.13) | collective-permute-done | bytes 32800 | tf_op jit(solution)/shard_map/cond/branch_6_fun/ppermute | solution.py:612
  50.8 0.0 all-to-all-done.6
  50.8 0.0 collective-permute-done.12
  50.8 3.4 %finish.1 = f32[4,128,256]{2,1,0:T(8,128)} custom-call(s32[1]{0:T(128)S(6)} %copy.43.turn_any.turn_ref, f32[32,8,128]{2,1,0:T(8,128)} %get-tuple-element.207.arr_any, f32[1184,128]{1,0:T(8,128)S(1)} %get-tuple-element.206.own_ref, f32[1184,128]{1,0:T(8,128)} %get-tuple-element.208.moved_ref, f32[64,128]{1,0:T(8,128)} %get-tuple-element.209.e_any, ...), custom_call_target="tpu_custom_call" | custom-call | tf_op jit(solution)/shard_map/finish/pallas_call | solution.py:556
Async XLA Ops:
  2.3 14.7 %collective-permute-start.14 = (f32[3,128,128]{2,1,0:T(8,128)}, f32[3,128,128]{2,1,0:T(8,128)S(1)}, u32[]{:S(2)}, u32[]{:S(2)}) collective-permute-start(f32[3,128,128]{2,1,0:T(8,128)} %get-tuple-element.199.hi_ref), channel_id=1, source_target_pairs={{0,1},{1,2},{2,3},{3,4},{4,5},{5,6},{6,7},{7,8},{8,9},{9,10},{10,1... | collective-permute-start | bytes 589832 | tf_op jit(solution)/shard_map/ppermute | solution.py:604
  4.4 12.6 %collective-permute-start.15 = (f32[3,128,128]{2,1,0:T(8,128)}, f32[3,128,128]{2,1,0:T(8,128)S(1)}, u32[]{:S(2)}, u32[]{:S(2)}) collective-permute-start(f32[3,128,128]{2,1,0:T(8,128)} %get-tuple-element.200.lo_ref), channel_id=1, source_target_pairs={{1,0},{2,1},{3,2},{4,3},{5,4},{6,5},{7,6},{8,7},{9,8},{10,9},{11,1... | collective-permute-start | bytes 589832 | tf_op jit(solution)/shard_map/ppermute | solution.py:605
  9.1 1.0 %copy-start = (f32[1,1,4,128,256]{4,3,2,1,0:T(8,128)S(1)}, f32[1,1,4,128,256]{4,3,2,1,0:T(8,128)}, u32[]{:S(2)}) copy-start(f32[1,1,4,128,256]{4,3,2,1,0:T(8,128)} %param.15) | copy-start | bytes 1572868
  10.1 10.4 %copy-start.1 = (f32[1,1,4,128,256]{4,3,2,1,0:T(8,128)S(1)}, f32[1,1,4,128,256]{4,3,2,1,0:T(8,128)}, u32[]{:S(2)}) copy-start(f32[1,1,4,128,256]{4,3,2,1,0:T(8,128)} %param.15) | copy-start | bytes 1572868
  10.1 10.4 %copy-start.3 = (f32[1,1,128,256]{3,2,1,0:T(8,128)S(1)}, f32[1,1,128,256]{3,2,1,0:T(8,128)}, u32[]{:S(2)}) copy-start(f32[1,1,128,256]{3,2,1,0:T(8,128)} %param.17) | copy-start | bytes 393220
  10.1 10.4 %copy-start.7 = (s32[1,1,4096]{2,1,0:T(1,128)S(1)}, s32[1,1,4096]{2,1,0:T(1,128)}, u32[]{:S(2)}) copy-start(s32[1,1,4096]{2,1,0:T(1,128)} %param.20) | copy-start | bytes 49156
  16.9 3.6 %copy-start.2 = (f32[1,1,2,128,256]{4,3,2,1,0:T(8,128)S(1)}, f32[1,1,2,128,256]{4,3,2,1,0:T(8,128)}, u32[]{:S(2)}) copy-start(f32[1,1,2,128,256]{4,3,2,1,0:T(8,128)} %param.16) | copy-start | bytes 786436
  17.0 11.1 %all-to-all-start.7 = ((f32[32,8,128]{2,1,0:T(8,128)}), f32[32,8,128]{2,1,0:T(8,128)S(1)}, u32[]{:S(2)}, u32[]{:S(2)}) async-start(f32[32,8,128]{2,1,0:T(8,128)} %interp.1), calls=%async_computation.7 | async-start | bytes 262144 | tf_op jit(solution)/shard_map/all_to_all | solution.py:574
  20.5 0.9 %copy-start.4 = (f32[3,128,128]{2,1,0:T(8,128)S(1)}, f32[3,128,128]{2,1,0:T(8,128)}, u32[]{:S(2)}) copy-start(f32[3,128,128]{2,1,0:T(8,128)} %get-tuple-element.200.lo_ref) | copy-start | bytes 589828
  21.5 0.9 %copy-start.5 = (f32[3,128,128]{2,1,0:T(8,128)S(1)}, f32[3,128,128]{2,1,0:T(8,128)}, u32[]{:S(2)}) copy-start(f32[3,128,128]{2,1,0:T(8,128)} %get-tuple-element.199.hi_ref) | copy-start | bytes 589828
  22.4 5.7 %copy-start.6 = (f32[1,1,3,4096]{3,1,2,0:T(1,128)S(1)}, f32[1,1,3,4096]{3,1,2,0:T(1,128)}, u32[]{:S(2)}) copy-start(f32[1,1,3,4096]{3,1,2,0:T(1,128)} %param.19) | copy-start | bytes 147460
  22.4 5.7 %copy-start.8 = (s32[1,1,4096]{2,1,0:T(1,128)S(1)}, s32[1,1,4096]{2,1,0:T(1,128)}, u32[]{:S(2)}) copy-start(s32[1,1,4096]{2,1,0:T(1,128)} %param.18) | copy-start | bytes 49156
  28.1 22.7 %collective-permute-start.12 = (f32[1184,128]{1,0:T(8,128)S(1)}, f32[1184,128]{1,0:T(8,128)}, u32[]{:S(2)}, u32[]{:S(2)}) collective-permute-start(f32[1184,128]{1,0:T(8,128)S(1)} %get-tuple-element.185), channel_id=1, source_target_pairs={{16,23},{17,24},{18,25},{19,26},{20,27},{21,28},{22,29},{23,30},{2... | collective-permute-start | bytes 1818632 | tf_op jit(solution)/shard_map/cond/branch_6_fun/ppermute | solution.py:612
  39.2 11.6 %all-to-all-start.6 = ((f32[32,8,128]{2,1,0:T(8,128)}), f32[32,8,128]{2,1,0:T(8,128)}, u32[]{:S(2)}, u32[]{:S(2)}) async-start(f32[32,8,128]{2,1,0:T(8,128)} %get-tuple-element.184), calls=%async_computation.6 | async-start | bytes 262144 | tf_op jit(solution)/shard_map/cond/branch_6_fun/all_to_all | solution.py:574
  42.6 8.2 %collective-permute-start.13 = (f32[64,128]{1,0:T(8,128)}, f32[64,128]{1,0:T(8,128)}, u32[]{:S(2)}, u32[]{:S(2)}) collective-permute-start(f32[64,128]{1,0:T(8,128)} %get-tuple-element.293), channel_id=1, source_target_pairs={{16,23},{17,24},{18,25},{19,26},{20,27},{21,28},{22,29},{23,30},{2... | collective-permute-start | bytes 98312 | tf_op jit(solution)/shard_map/cond/branch_6_fun/ppermute | solution.py:612

commit v3 on v2

--- a/solution.py
+++ b/solution.py
@@ -112,6 +112,20 @@
     return out
 
 
+def fold(v):
+    n = v.shape[0] // 4
+    tail = jnp.concatenate([pltpu.roll(v[3*n:], 128 - CY - i * CY, axis=1) for i in range(3)], axis=0)
+    lane = lax.broadcasted_iota(jnp.int32, tail.shape, 1)
+    return jnp.where(lane < 3 * CY, v[:3*n], tail)
+
+
+def unfold3(v):
+    n = v.shape[0] // 3
+    a, b, c = [pltpu.roll(v[i*n:(i+1)*n], (i + 1) * CY, axis=1) for i in range(3)]
+    lane = lax.broadcasted_iota(jnp.int32, a.shape, 1)
+    return jnp.concatenate([v, jnp.where(lane < CY, a, jnp.where(lane < 2 * CY, b, c))], axis=0)
+
+
 def pack_kernel(f_any, kap_any, al_any, lo_any, hi_any, f_ref, kap_ref, al_ref, lo_ref, hi_ref, sems):
     nf, nz, npl = f_ref.shape
     copies = [pltpu.make_async_copy(f_any.at[f], f_ref.at[f], sems.at[f]) for f in range(nf)]
@@ -130,19 +144,20 @@
         return kap_ref[f, :, sl] if f < 2 else al_ref[:, sl]
 
     sides = ((lo_ref, lo_any, 0, 0, 1), (hi_ref, hi_any, nt - 1, per - 1, -1))
-    back = [pltpu.make_async_copy(ref.at[j], out.at[j], sems.at[nf + 3 + 3 * i + j])
-            for i, (ref, out, *_) in enumerate(sides) for j in range(3)]
+    parts = [slice(0, nz), slice(nz, 2 * nz), slice(2 * nz, 2 * nz + nz * 3 // 4)]
+    back = [pltpu.make_async_copy(ref.at[p], out.at[p], sems.at[nf + 3 + 3 * i + j])
+            for i, (ref, out, *_) in enumerate(sides) for j, p in enumerate(parts)]
     for c in copies[:nf]:
         c.wait()
     for i, (ref, _, t, x, step) in enumerate(sides):
-        ref[0] = pack_planes(field, nf, t, x, lane)
+        ref[parts[0]] = pack_planes(field, nf, t, x, lane)
         back[3 * i].start()
-        ref[1] = pack_planes(field, nf, t, x + step, lane)
+        ref[parts[1]] = pack_planes(field, nf, t, x + step, lane)
         back[3 * i + 1].start()
     for c in copies[nf:]:
         c.wait()
     for i, (ref, _, t, x, step) in enumerate(sides):
-        ref[2] = pack_planes(coef, 3, t, x, lane)
+        ref[parts[2]] = fold(pack_planes(coef, 3, t, x, lane))
         back[3 * i + 2].start()
     for c in back:
         c.wait()
@@ -150,7 +165,7 @@
 
 def pack(fields, kappa, along):
     nf, nz, npl = fields.shape
-    sh = jax.ShapeDtypeStruct((3, nz, nf * CY), F32)
+    sh = jax.ShapeDtypeStruct((2 * nz + nz * 3 // 4, nf * CY), F32)
     return pl.pallas_call(
         pack_kernel,
         out_shape=(sh, sh),
@@ -170,7 +185,7 @@
     return by, tiles * (1 - back), lax.rem(me + turn * back, blocks), back, lax.rem(me + blocks - turn * back, blocks)
 
 
-def load_tiles(unroll, o_ref, info_ref, base_ref, frac_ref, a_ref, shift, nf, nz, npl, tile):
+def load_tiles(unroll, o_ref, info_ref, base_ref, frac_ref, a_ref, shift, nf, nz, npl, tile, t_ref=None):
     nx = npl // CY
     nt = base_ref.shape[1] // tile
     o_ref[pl.ds(nt - info_ref[1], nt)] = jnp.zeros((nt,) + o_ref.shape[1:], F32)
@@ -190,13 +205,29 @@
         wy = jnp.where(iy == y0, 1.0 - fy, jnp.where(iy == y0 + 1, fy, 0.0))
         wx = [jnp.where(x0 == x, 1.0 - fx, jnp.where(x0 == x - 1, fx, 0.0)) for x in range(nx)]
         rows = []
-        for f in range(nf):
+        for f in range(nf if t_ref is None else nf - 1):
             p = jnp.dot(a_ref[f * npl:(f + 1) * npl, :], w, preferred_element_type=F32)
             acc = wx[0] * p[:CY]
             for x in range(1, nx):
                 acc = acc + wx[x] * p[x * CY:(x + 1) * CY]
             r = jnp.sum(acc * wy, axis=0, keepdims=True)
             rows += [r[:, i * 128:(i + 1) * 128] for i in range(tile // 128)]
+        for i in range(tile // 128 if t_ref is not None else 0):
+            sl = slice(i * 128, (i + 1) * 128)
+            low = jnp.broadcast_to(z0[:, sl], (8, 128))
+            high = low + 1
+            total = None
+            for y in range(0, CY, 8):
+                at0 = at1 = None
+                for x in range(nx):
+                    v = t_ref[x * CY + y:x * CY + y + 8, :]
+                    v0 = wx[x][:, sl] * jnp.take_along_axis(v, low, axis=1)
+                    v1 = wx[x][:, sl] * jnp.take_along_axis(v, high, axis=1)
+                    at0 = v0 if at0 is None else at0 + v0
+                    at1 = v1 if at1 is None else at1 + v1
+                v = (at0 * (1.0 - fz[:, sl]) + at1 * fz[:, sl]) * wy[y:y + 8, sl]
+                total = v if total is None else total + v
+            rows.append(jnp.sum(total, axis=0, keepdims=True))
         o_ref[info_ref[1] + t] = jnp.concatenate(rows, axis=0)
         return carry
 
@@ -210,18 +241,15 @@
         a_ref[row:row + n, i * nz:(i + 1) * nz] = part
 
 
-def interp_kernel(turn_any, f_any, base_any, frac_any, o_ref, a_ref, f_ref, base_ref, frac_ref, turn_ref, sems, *, tile, blocks, turned):
+def interp_kernel(turn_any, f_ref, base_any, frac_any, o_ref, a_ref, base_ref, frac_ref, turn_ref, sems, *, tile, blocks, turned):
     nf, nz, npl = f_ref.shape
-    copies = [pltpu.make_async_copy(f_any.at[f], f_ref.at[f], sems.at[f]) for f in range(nf)]
-    copies += [pltpu.make_async_copy(base_any, base_ref, sems.at[nf])]
-    copies += [pltpu.make_async_copy(frac_any, frac_ref, sems.at[nf + 1])]
-    copies += [pltpu.make_async_copy(turn_any, turn_ref, sems.at[nf + 2])]
+    pairs = ((base_any, base_ref), (frac_any, frac_ref), (turn_any, turn_ref))
+    copies = [pltpu.make_async_copy(a, b, sems.at[i]) for i, (a, b) in enumerate(pairs)]
     for c in copies:
         c.start()
     for f in range(nf):
-        copies[f].wait()
         split_into(a_ref, f * npl, f_ref[f].T)
-    for c in copies[nf:]:
+    for c in copies:
         c.wait()
     info_ref = places(turn_ref[0], base_ref.shape[1] // tile, blocks, turned)
     load_tiles(16, o_ref, info_ref, base_ref, frac_ref, a_ref, info_ref[0], nf, nz, npl, tile)
@@ -233,11 +261,11 @@
     return pl.pallas_call(
         functools.partial(interp_kernel, tile=tile, blocks=blocks, turned=turned),
         out_shape=jax.ShapeDtypeStruct((2 * slots // tile, nf * tile // 128, 128), F32),
-        in_specs=[ANY] * 4,
+        in_specs=[ANY, VM, ANY, ANY],
         out_specs=VM,
-        scratch_shapes=[pltpu.VMEM((nf * npl, 4 * nz), BF), pltpu.VMEM(fields.shape, F32),
+        scratch_shapes=[pltpu.VMEM((nf * npl, 4 * nz), BF),
                         pltpu.VMEM(base.shape, jnp.int32), pltpu.VMEM(frac.shape, F32),
-                        pltpu.SMEM((1,), jnp.int32), pltpu.SemaphoreType.DMA((nf + 3,))],
+                        pltpu.SMEM((1,), jnp.int32), pltpu.SemaphoreType.DMA((3,))],
         compiler_params=CP,
         name="interp",
     )(turn, fields, base, frac)
@@ -276,16 +304,16 @@
         g[:, k*npl:(k+1)*npl] = 2.0 + (1.0 + 4.0 * kap_ref[k]) * inv
     outer = []
     for i, (near, mine) in enumerate(((left_ref, lo_ref), (right_ref, hi_ref))):
-        c3 = near[2]
+        c3 = unfold3(near[2*nz:, :])
         r32, r64, r96 = [pltpu.roll(c3, j, axis=1) for j in (32, 64, 96)]
         c = jnp.where(lane < CY, c3, jnp.where(lane < 2*CY, r32, r64))
         s = jnp.where(lane < CY, r64, jnp.where(lane < 2*CY, r96, jnp.where(lane < 3*CY, c3, r32)))
         inv = 1.0 / s
         g[:, own+i*128:own+(i+1)*128] = 2.0 + (1.0 + 4.0 * c) * inv
-        v = near[0]
+        v = near[:nz, :]
         z = jnp.where(fringe, 0.0, v)
         side = pltpu.roll(z, 1, axis=1) + pltpu.roll(z, 127, axis=1)
-        outer.append((v + c * (near[1] + mine[0] + side)) * inv)
+        outer.append((v + c * (near[nz:2*nz, :] + mine[:nz, :] + side)) * inv)
     fs = (q0, q1, p1, q2, p2)
     factor(g, q0, q1, p1, q2, p2, h, iv)
 
@@ -293,7 +321,7 @@
         return jnp.where(fringe, 0.0, v)
 
     right_sides(start_ref, lambda f: [clear(start_ref[f, :, t*128:(t+1)*128]) for t in range(nt)],
-                left_ref[0], right_ref[0], kap_ref, si, y, fs, lane)
+                left_ref[:nz, :], right_ref[:nz, :], kap_ref, si, y, fs, lane)
     for i in range(2):
         y[:, nf*npl+i*128:nf*npl+(i+1)*128] = reduce_rhs(outer[i], slice(own+i*128, own+(i+1)*128), fs)
 
@@ -399,7 +427,7 @@
     return k // nq % nf * npl + k % nq // 2 * CY + jnp.where(k % 2 == 0, low, high)
 
 
-def relay_kernel(turn_ref, arr_ref, cells_ref, f1t_ref, fac_ref, base_ref, frac_ref, o_ref, e_ref, a_ref, ys, *, tile, nf, edges, blocks, turned):
+def relay_kernel(turn_ref, arr_ref, cells_ref, f1t_ref, fac_ref, base_ref, frac_ref, o_ref, e_ref, a_ref, ys, t_ref, *, tile, nf, edges, blocks, turned):
     nz = f1t_ref.shape[1]
     info_ref = places(turn_ref[0], base_ref.shape[1] // tile, blocks, turned)
     npl = f1t_ref.shape[0] // nf
@@ -427,8 +455,12 @@
         row = lax.broadcasted_iota(jnp.int32, (npl, 256), 0) + f * npl
         put = (row == target).astype(F32).astype(BF)
         add = lax.dot_general(put, terms, (((1,), (1,)), ((), ())), preferred_element_type=F32)
-        split_into(a_ref, f * npl, f1t_ref[f*npl:(f+1)*npl, :] + add)
-    load_tiles(UNROLL, o_ref, info_ref, base_ref, frac_ref, a_ref, None, nf, nz, npl, tile)
+        v = f1t_ref[f*npl:(f+1)*npl, :] + add
+        if f < nf - 1:
+            split_into(a_ref, f * npl, v)
+        else:
+            t_ref[...] = v
+    load_tiles(UNROLL, o_ref, info_ref, base_ref, frac_ref, a_ref, None, nf, nz, npl, tile, t_ref)
     if edges:
         turned = e.T
         nt = slots // tile
@@ -445,7 +477,8 @@
         out_shape=(jax.ShapeDtypeStruct(arrived.shape, F32), jax.ShapeDtypeStruct((nz // 2, 128), F32)),
         in_specs=[SM] + [VM] * 6,
         out_specs=(VM, VM),
-        scratch_shapes=[pltpu.VMEM((f1t.shape[0], 4 * nz), BF), pltpu.VMEM((nz, 128), F32)],
+        scratch_shapes=[pltpu.VMEM((f1t.shape[0], 4 * nz), BF), pltpu.VMEM((nz, 128), F32),
+                        pltpu.VMEM((f1t.shape[0] // nf, nz), F32)],
         compiler_params=CP,
         name="relay",
     )(turn, arrived, cells, f1t, fac, base, frac)
@@ -494,15 +527,15 @@
     held = copies(own_ref, e_any)
     lane = lanes(nz)
     q = lane % nq
+    came.wait()
     held[0].wait()
+    held[2].wait()
     ln = lane % half
     few = ln // nq // (nf - 1) * 2 * nq + lane // half * nq + ln % nq
     table = pay_ref[j*nz:(j+1)*nz, :]
     cs = jnp.take_along_axis(table, few, axis=1)
     gs[...] = jnp.take_along_axis(table, few + half, axis=1)
     factor(gs, *fac)
-    came.wait()
-    held[2].wait()
     e = unfold(e_ref[...])
     if edges:
         chunks = arr_ref.shape[0] // 2

time: 54.8 us -> 54.5 us (level)
  waiting for transfers between devices: 5.33 us -> 6.77 us
  starting transfers between devices: 21.3 us -> 20.2 us
  Pallas kernels: 23.8 us -> 22.8 us
    ppermute x2, starting transfers between devices: 8.25 us -> 6.79 us  [shift(): return lax.ppermute(v, ('mesh', 'blk'), pairs)]
    ppermute x2, waiting for transfers between devices: 3.08 us -> 4.46 us  [shift(): return lax.ppermute(v, ('mesh', 'blk'), pairs)]
  transfers between devices with their start and end apart: 6 -> 6, of which waited for: 2 -> 2; matrix products, arithmetic and copies ran while one was open for 0% -> 0% of each run, Pallas kernels for 33% -> 32%
where the time goes in v3:
time: 54.5 us; the launch traced here: 53.7 us
  Pallas kernels  22.8 us (42%)
  starting transfers between devices  20.2 us (37%)
  waiting for transfers between devices  6.77 us (12%)
  local copies, waits for them, and re-layouts  2.9 us (5%)
  between operations  0.95 us (2%)
    pallas_call x1, Pallas kernels, relay(): pl.pallas_call(functools.partial(relay_kernel, tile=tile, nf=nf, edges=ed...  7.45 us
    all_to_all x2, starting transfers between devices, exchange(): return lax.all_to_all(values, ('mesh', 'blk'), 0, 0, tiled=True)  7.31 us
    ppermute x2, starting transfers between devices, shift(): return lax.ppermute(v, ('mesh', 'blk'), pairs)  6.79 us
    pallas_call x1, Pallas kernels, interp(): pl.pallas_call(functools.partial(interp_kernel, tile=tile, blocks=blocks,...  6.29 us
    ppermute x2, waiting for transfers between devices, shift(): return lax.ppermute(v, ('mesh', 'blk'), pairs)  4.46 us
    ppermute x1, starting transfers between devices, local(): lax.ppermute(low, 'blk', [((i + 1) % blocks, i) for i in range(blocks)])  4.06 us
    pallas_call x1, Pallas kernels, march(): pl.pallas_call(march_kernel, out_shape=(jax.ShapeDtypeStruct((nf * npl, n...  3.49 us
    pallas_call x1, Pallas kernels, finish(): pl.pallas_call(functools.partial(finish_kernel, edges=len(e) == 2, blocks...  3.24 us
  transfers between devices with their start and end apart: 6, of which 2 were waited for; matrix products, arithmetic and copies ran while one was open for 0% of the time, Pallas kernels for 32%

profile of v3, /device:TPU:1, one launch (start us, length us, event | category | flops | bytes accessed | tf_op | source)
XLA Modules:
  0.0 53.7 jit_solution(18380297534497195936)
XLA Ops:
  0.0 2.3 %pack.1 = (f32[352,128]{1,0:T(8,128)}, f32[352,128]{1,0:T(8,128)}) custom-call(f32[4,128,256]{2,1,0:T(8,128)} %bitcast.43, f32[2,128,256]{2,1,0:T(8,128)} %bitcast.46, f32[128,256]{1,0:T(8,128)} %bitcast.48), custom_call_target="tpu_custom_call" | custom-call | tf_op jit(solution)/shard_map/pack/pallas_call | solution.py:169
  2.3 2.1 %collective-permute-start.14 = (f32[352,128]{1,0:T(8,128)}, f32[352,128]{1,0:T(8,128)S(1)}, u32[]{:S(2)}, u32[]{:S(2)}) collective-permute-start(f32[352,128]{1,0:T(8,128)} %get-tuple-element.199.hi_ref), channel_id=1, source_target_pairs={{0,1},{1,2},{2,3},{3,4},{4,5},{5,6},{6,7},{7,8},{8,9},{9,10},{10,1... | collective-permute-start | bytes 540680 | tf_op jit(solution)/shard_map/ppermute | solution.py:637
  4.4 4.1 %collective-permute-start.15 = (f32[352,128]{1,0:T(8,128)}, f32[352,128]{1,0:T(8,128)S(1)}, u32[]{:S(2)}, u32[]{:S(2)}) collective-permute-start(f32[352,128]{1,0:T(8,128)} %get-tuple-element.200.lo_ref), channel_id=1, source_target_pairs={{1,0},{2,1},{3,2},{4,3},{5,4},{6,5},{7,6},{8,7},{9,8},{10,9},{11,1... | collective-permute-start | bytes 540680 | tf_op jit(solution)/shard_map/ppermute | solution.py:638
  9.1 0.0 copy-start
  9.1 1.0 %copy-done = f32[1,1,4,128,256]{4,3,2,1,0:T(8,128)S(1)} copy-done((f32[1,1,4,128,256]{4,3,2,1,0:T(8,128)S(1)}, f32[1,1,4,128,256]{4,3,2,1,0:T(8,128)}, u32[]{:S(2)}) %copy-start) | copy-done | bytes 524312
  10.2 0.0 copy-start.1
  10.2 0.0 copy-start.3
  10.2 0.0 copy-start.7
  10.2 6.3 %interp.1 = f32[32,8,128]{2,1,0:T(8,128)} custom-call(s32[1]{0:T(128)S(6)} %copy.43.turn_any.turn_ref, f32[4,128,256]{2,1,0:T(8,128)S(1)} %bitcast.44, s32[1,4096]{1,0:T(1,128)} %bitcast.66, f32[3,1,4096]{2,1,0:T(1,128)} %bitcast.50), custom_call_target="tpu_custom_call" | custom-call | tf_op jit(solution)/shard_map/interp/pallas_call | solution.py:261
  16.5 0.0 copy-start.2
  16.5 0.0 collective-permute-done.14.left_ref
  16.5 0.0 collective-permute-done.15.right_ref
  16.5 3.3 %all-to-all-start.7 = ((f32[32,8,128]{2,1,0:T(8,128)}), f32[32,8,128]{2,1,0:T(8,128)S(1)}, u32[]{:S(2)}, u32[]{:S(2)}) async-start(f32[32,8,128]{2,1,0:T(8,128)} %interp.1), calls=%async_computation.7 | async-start | bytes 262144 | tf_op jit(solution)/shard_map/all_to_all | solution.py:607
  19.9 0.0 copy-done.1
  19.9 0.0 copy-done.3
  19.9 0.0 copy-done.7
  19.9 0.0 copy-done.2
  19.9 0.0 copy-start.4
  19.9 0.9 %copy-done.4 = f32[352,128]{1,0:T(8,128)S(1)} copy-done((f32[352,128]{1,0:T(8,128)S(1)}, f32[352,128]{1,0:T(8,128)}, u32[]{:S(2)}) %copy-start.4) | copy-done | bytes 180248
  20.8 0.0 copy-start.5
  20.8 0.9 %copy-done.5 = f32[352,128]{1,0:T(8,128)S(1)} copy-done((f32[352,128]{1,0:T(8,128)S(1)}, f32[352,128]{1,0:T(8,128)}, u32[]{:S(2)}) %copy-start.5) | copy-done | bytes 180248
  21.7 0.0 copy-start.6
  21.7 0.0 copy-start.8
  21.7 3.5 %march.1 = (f32[1024,128]{1,0:T(8,128)S(1)}, f32[1184,128]{1,0:T(8,128)S(1)}, f32[1024,128]{1,0:T(8,128)S(1)}) custom-call(f32[4,128,256]{2,1,0:T(8,128)S(1)} %bitcast.45, f32[2,128,256]{2,1,0:T(8,128)S(1)} %bitcast.47, f32[128,256]{1,0:T(8,128)S(1)} %bitcast.49, f32[352,128]{1,0:T(8,128)S(1)} %copy-done.4, f32[352,128]{1,0:T(8,128)S(1)} %copy-done.5, ...), custom_call_target="tpu_custom_call" | custom-call | tf_op jit(solution)/shard_map/march/pallas_call | solution.py:385
  25.2 2.3 %all-to-all-done.7 = f32[32,8,128]{2,1,0:T(8,128)S(1)} async-done(((f32[32,8,128]{2,1,0:T(8,128)}), f32[32,8,128]{2,1,0:T(8,128)S(1)}, u32[]{:S(2)}, u32[]{:S(2)}) %all-to-all-start.7) | async-done | bytes 131104 | tf_op jit(solution)/shard_map/all_to_all | solution.py:607
  27.5 0.0 copy-done.6
  27.5 0.0 copy-done.8
  27.5 22.7 %conditional.1 = (f32[32,8,128]{2,1,0:T(8,128)}, f32[1184,128]{1,0:T(8,128)}, f32[64,128]{1,0:T(8,128)}, f32[64,128]{1,0:T(8,128)}) conditional(s32[]{:T(128)} %bitcast.35, (s32[1,1,4096]{2,1,0:T(1,128)S(1)}, s32[1,1,4096]{2,1,0:T(1,128)S(1)}, f32[1,1,3,4096]{3,1,2,0:T(1,128)S(1)}, s32[1]{0:T(128)}, ...), branch_computations={%region_0.0_spmd, %region_1.0_spmd, %region_2.0_spmd, %region_3.0_... | conditional | bytes 2949264 | solution.py:662
  27.5 2.6 %collective-permute-start.10 = (f32[1184,128]{1,0:T(8,128)S(1)}, f32[1184,128]{1,0:T(8,128)}, u32[]{:S(2)}, u32[]{:S(2)}) collective-permute-start(f32[1184,128]{1,0:T(8,128)S(1)} %get-tuple-element.175), channel_id=1, source_target_pairs={{16,22},{17,23},{18,24},{19,25},{20,26},{21,27},{22,28},{23,29},{2... | collective-permute-start | bytes 1818632 | tf_op jit(solution)/shard_map/cond/branch_5_fun/ppermute | solution.py:645
  30.1 7.5 %relay.12 = (f32[32,8,128]{2,1,0:T(8,128)}, f32[64,128]{1,0:T(8,128)}) custom-call(s32[1]{0:T(128)} %get-tuple-element.167.turn_ref, f32[32,8,128]{2,1,0:T(8,128)S(1)} %get-tuple-element.168.arr_ref, s32[1,4096]{1,0:T(1,128)S(1)} %bitcast.64, f32[1024,128]{1,0:T(8,128)S(1)} %get-tuple-element.170.f1t_ref, f32[1024,128]{1,0:T(8,128)S(1)} %get-tuple-element.171.fac_ref, ...), custom_call_target="tpu_custom_call" | custom-call | tf_op jit(solution)/shard_map/cond/branch_5_fun/relay/pallas_call | solution.py:475
  37.6 4.0 %all-to-all-start.5 = ((f32[32,8,128]{2,1,0:T(8,128)}), f32[32,8,128]{2,1,0:T(8,128)}, u32[]{:S(2)}, u32[]{:S(2)}) async-start(f32[32,8,128]{2,1,0:T(8,128)} %get-tuple-element.174), calls=%async_computation.5 | async-start | bytes 262144 | tf_op jit(solution)/shard_map/cond/branch_5_fun/all_to_all | solution.py:607
  41.6 4.2 %collective-permute-start.11 = (f32[64,128]{1,0:T(8,128)}, f32[64,128]{1,0:T(8,128)}, u32[]{:S(2)}, u32[]{:S(2)}) collective-permute-start(f32[64,128]{1,0:T(8,128)} %get-tuple-element.289), channel_id=1, source_target_pairs={{16,22},{17,23},{18,24},{19,25},{20,26},{21,27},{22,28},{23,29},{2... | collective-permute-start | bytes 98312 | tf_op jit(solution)/shard_map/cond/branch_5_fun/ppermute | solution.py:645
  45.8 4.5 %collective-permute-done.11 = f32[64,128]{1,0:T(8,128)} collective-permute-done((f32[64,128]{1,0:T(8,128)}, f32[64,128]{1,0:T(8,128)}, u32[]{:S(2)}, u32[]{:S(2)}) %collective-permute-start.11) | collective-permute-done | bytes 32800 | tf_op jit(solution)/shard_map/cond/branch_5_fun/ppermute | solution.py:645
  50.3 0.0 all-to-all-done.5
  50.3 0.0 collective-permute-done.10
  50.3 3.2 %finish.1 = f32[4,128,256]{2,1,0:T(8,128)} custom-call(s32[1]{0:T(128)S(6)} %copy.43.turn_any.turn_ref, f32[32,8,128]{2,1,0:T(8,128)} %get-tuple-element.207.arr_any, f32[1184,128]{1,0:T(8,128)S(1)} %get-tuple-element.206.own_ref, f32[1184,128]{1,0:T(8,128)} %get-tuple-element.208.moved_ref, f32[64,128]{1,0:T(8,128)} %get-tuple-element.209.e_any, ...), custom_call_target="tpu_custom_call" | custom-call | tf_op jit(solution)/shard_map/finish/pallas_call | solution.py:589
Async XLA Ops:
  2.3 14.2 %collective-permute-start.14 = (f32[352,128]{1,0:T(8,128)}, f32[352,128]{1,0:T(8,128)S(1)}, u32[]{:S(2)}, u32[]{:S(2)}) collective-permute-start(f32[352,128]{1,0:T(8,128)} %get-tuple-element.199.hi_ref), channel_id=1, source_target_pairs={{0,1},{1,2},{2,3},{3,4},{4,5},{5,6},{6,7},{7,8},{8,9},{9,10},{10,1... | collective-permute-start | bytes 540680 | tf_op jit(solution)/shard_map/ppermute | solution.py:637
  4.4 12.1 %collective-permute-start.15 = (f32[352,128]{1,0:T(8,128)}, f32[352,128]{1,0:T(8,128)S(1)}, u32[]{:S(2)}, u32[]{:S(2)}) collective-permute-start(f32[352,128]{1,0:T(8,128)} %get-tuple-element.200.lo_ref), channel_id=1, source_target_pairs={{1,0},{2,1},{3,2},{4,3},{5,4},{6,5},{7,6},{8,7},{9,8},{10,9},{11,1... | collective-permute-start | bytes 540680 | tf_op jit(solution)/shard_map/ppermute | solution.py:638
  9.1 1.0 %copy-start = (f32[1,1,4,128,256]{4,3,2,1,0:T(8,128)S(1)}, f32[1,1,4,128,256]{4,3,2,1,0:T(8,128)}, u32[]{:S(2)}) copy-start(f32[1,1,4,128,256]{4,3,2,1,0:T(8,128)} %param.15) | copy-start | bytes 1572868
  10.2 9.7 %copy-start.1 = (f32[1,1,4,128,256]{4,3,2,1,0:T(8,128)S(1)}, f32[1,1,4,128,256]{4,3,2,1,0:T(8,128)}, u32[]{:S(2)}) copy-start(f32[1,1,4,128,256]{4,3,2,1,0:T(8,128)} %param.15) | copy-start | bytes 1572868
  10.2 9.7 %copy-start.3 = (f32[1,1,128,256]{3,2,1,0:T(8,128)S(1)}, f32[1,1,128,256]{3,2,1,0:T(8,128)}, u32[]{:S(2)}) copy-start(f32[1,1,128,256]{3,2,1,0:T(8,128)} %param.17) | copy-start | bytes 393220
  10.2 9.7 %copy-start.7 = (s32[1,1,4096]{2,1,0:T(1,128)S(1)}, s32[1,1,4096]{2,1,0:T(1,128)}, u32[]{:S(2)}) copy-start(s32[1,1,4096]{2,1,0:T(1,128)} %param.20) | copy-start | bytes 49156
  16.5 3.4 %copy-start.2 = (f32[1,1,2,128,256]{4,3,2,1,0:T(8,128)S(1)}, f32[1,1,2,128,256]{4,3,2,1,0:T(8,128)}, u32[]{:S(2)}) copy-start(f32[1,1,2,128,256]{4,3,2,1,0:T(8,128)} %param.16) | copy-start | bytes 786436
  16.5 11.0 %all-to-all-start.7 = ((f32[32,8,128]{2,1,0:T(8,128)}), f32[32,8,128]{2,1,0:T(8,128)S(1)}, u32[]{:S(2)}, u32[]{:S(2)}) async-start(f32[32,8,128]{2,1,0:T(8,128)} %interp.1), calls=%async_computation.7 | async-start | bytes 262144 | tf_op jit(solution)/shard_map/all_to_all | solution.py:607
  19.9 0.9 %copy-start.4 = (f32[352,128]{1,0:T(8,128)S(1)}, f32[352,128]{1,0:T(8,128)}, u32[]{:S(2)}) copy-start(f32[352,128]{1,0:T(8,128)} %get-tuple-element.200.lo_ref) | copy-start | bytes 540676
  20.8 0.9 %copy-start.5 = (f32[352,128]{1,0:T(8,128)S(1)}, f32[352,128]{1,0:T(8,128)}, u32[]{:S(2)}) copy-start(f32[352,128]{1,0:T(8,128)} %get-tuple-element.199.hi_ref) | copy-start | bytes 540676
  21.7 5.8 %copy-start.6 = (f32[1,1,3,4096]{3,1,2,0:T(1,128)S(1)}, f32[1,1,3,4096]{3,1,2,0:T(1,128)}, u32[]{:S(2)}) copy-start(f32[1,1,3,4096]{3,1,2,0:T(1,128)} %param.19) | copy-start | bytes 147460
  21.7 5.8 %copy-start.8 = (s32[1,1,4096]{2,1,0:T(1,128)S(1)}, s32[1,1,4096]{2,1,0:T(1,128)}, u32[]{:S(2)}) copy-start(s32[1,1,4096]{2,1,0:T(1,128)} %param.18) | copy-start | bytes 49156
  27.5 22.7 %collective-permute-start.10 = (f32[1184,128]{1,0:T(8,128)S(1)}, f32[1184,128]{1,0:T(8,128)}, u32[]{:S(2)}, u32[]{:S(2)}) collective-permute-start(f32[1184,128]{1,0:T(8,128)S(1)} %get-tuple-element.175), channel_id=1, source_target_pairs={{16,22},{17,23},{18,24},{19,25},{20,26},{21,27},{22,28},{23,29},{2... | collective-permute-start | bytes 1818632 | tf_op jit(solution)/shard_map/cond/branch_5_fun/ppermute | solution.py:645
  37.6 12.7 %all-to-all-start.5 = ((f32[32,8,128]{2,1,0:T(8,128)}), f32[32,8,128]{2,1,0:T(8,128)}, u32[]{:S(2)}, u32[]{:S(2)}) async-start(f32[32,8,128]{2,1,0:T(8,128)} %get-tuple-element.174), calls=%async_computation.5 | async-start | bytes 262144 | tf_op jit(solution)/shard_map/cond/branch_5_fun/all_to_all | solution.py:607
  41.6 8.7 %collective-permute-start.11 = (f32[64,128]{1,0:T(8,128)}, f32[64,128]{1,0:T(8,128)}, u32[]{:S(2)}, u32[]{:S(2)}) collective-permute-start(f32[64,128]{1,0:T(8,128)} %get-tuple-element.289), channel_id=1, source_target_pairs={{16,22},{17,23},{18,24},{19,25},{20,26},{21,27},{22,28},{23,29},{2... | collective-permute-start | bytes 98312 | tf_op jit(solution)/shard_map/cond/branch_5_fun/ppermute | solution.py:645

commit v4 on v3

--- a/solution.py
+++ b/solution.py
@@ -368,9 +368,11 @@
     gg = 2.0 + (inv + 4.0 * cs)
     j = nf * nt
     few = (lane // (4 * nx) % 2) * (nf - 1) * 2 * nx + (lane // (2 * nx) % 2) * half + ln % (2 * nx)
-    pay_ref[j*nz:(j+1)*nz, :] = jnp.where(
-        lane < half, jnp.take_along_axis(cs, few, axis=1), jnp.take_along_axis(gg, few, axis=1))
-    pay_ref[(j+1)*nz:, :] = cells_ref[...].astype(F32)
+    one = (lane - half) // (2 * nx) % 2 * half + ln % (2 * nx)
+    table = jnp.where(lane < half, jnp.take_along_axis(cs, few, axis=1), jnp.take_along_axis(inv, one, axis=1))
+    kept = cells_ref[...].astype(F32)
+    kept = jnp.concatenate([jnp.zeros((128 - kept.shape[0], nz), F32), kept], axis=0).T
+    pay_ref[j*nz:(j+1)*nz, :] = jnp.where(lane < half + 4 * nx, table, kept)
     gs[...] = gg
     refs = [fac_ref.at[i*nz:(i+1)*nz] for i in range(7)]
     factor(gs, *refs)
@@ -380,7 +382,8 @@
 def march(start, kappa, along, low, high, left, right, cells):
     nf, nz, npl = start.shape
     nt = npl // 128
-    rows = (nf * nt + 1) * nz + cells.shape[0]
+    assert cells.shape[0] <= 128 - nf * 2 * npl // CY - 4 * npl // CY
+    rows = (nf * nt + 1) * nz
     w = 2 * npl + 256
     return pl.pallas_call(
         march_kernel,
@@ -493,15 +496,15 @@
         out_any, *refs = refs
     else:
         el_ref, er_ref, out_any, *refs = refs
-    arr_ref, e_ref, o_ref, pay_ref, ys, gs, *fac, sems = refs
+    arr_ref, e_ref, o_ref, pay_ref, turned_ref, ys, gs, *fac, sems = refs
     nf, nz, npl = o_ref.shape
     nt = npl // 128
     nx = npl // CY
     nq = 2 * nx
     half = nf * nq
     j = nf * nt
-    cells0 = (j + 1) * nz
-    slots = (pay_ref.shape[0] - cells0) * 128
+    slots = arr_ref.shape[0] // 2 * arr_ref.shape[1] // nf * 128
+    cells0 = 128 - slots // 128
     lines = slice(j * nz, pay_ref.shape[0])
     rest = slice(0, j * nz)
     came = pltpu.make_async_copy(arr_any, arr_ref, sems.at[2])
@@ -534,7 +537,9 @@
     few = ln // nq // (nf - 1) * 2 * nq + lane // half * nq + ln % nq
     table = pay_ref[j*nz:(j+1)*nz, :]
     cs = jnp.take_along_axis(table, few, axis=1)
-    gs[...] = jnp.take_along_axis(table, few + half, axis=1)
+    inv = jnp.take_along_axis(table, half + lane // half * nq + ln % nq, axis=1)
+    gs[...] = 2.0 + (inv + 4.0 * cs)
+    turned_ref[...] = table.T
     factor(gs, *fac)
     e = unfold(e_ref[...])
     if edges:
@@ -557,7 +562,7 @@
 
     def cell_row(g, tile):
         per = tile // 128
-        rows = [pay_ref[pl.ds(cells0 + g * per + i, 1), :] for i in range(per)]
+        rows = [turned_ref[pl.ds(cells0 + g * per + i, 1), :] for i in range(per)]
         return jnp.concatenate(rows, axis=1).astype(jnp.int32)
 
     sm = place_small(info_ref[0], arr_ref, info_ref[1], cell_row, slots, nf, nz, npl)
@@ -592,7 +597,7 @@
         in_specs=[SM] + [ANY] * 5 + [VM] * (len(e) - 2),
         out_specs=ANY,
         scratch_shapes=[pltpu.VMEM(v.shape, F32) for v in (arrived, e[0])] + [pltpu.VMEM(shape, F32), pltpu.VMEM(own.shape, F32)]
-        + [pltpu.VMEM((nz, 128), F32)] * 9 + [pltpu.SemaphoreType.DMA((4 + shape[0],))],
+        + [pltpu.VMEM((nz, 128), F32)] * 10 + [pltpu.SemaphoreType.DMA((4 + shape[0],))],
         compiler_params=CP,
         name="finish",
     )(turn, arrived, own, moved, *e)

time: 54.5 us -> 53.9 us (0.989)
  no operation moved by 1% of the time
where the time goes in v4:
time: 53.9 us; the launch traced here: 53.5 us
  Pallas kernels  22.9 us (42%)
  starting transfers between devices  20.2 us (37%)
  waiting for transfers between devices  6.41 us (12%)
  local copies, waits for them, and re-layouts  2.9 us (5%)
  between operations  0.95 us (2%)
    pallas_call x1, Pallas kernels, relay(): pl.pallas_call(functools.partial(relay_kernel, tile=tile, nf=nf, edges=ed...  7.45 us
    all_to_all x2, starting transfers between devices, exchange(): return lax.all_to_all(values, ('mesh', 'blk'), 0, 0, tiled=True)  7.31 us
    ppermute x2, starting transfers between devices, shift(): return lax.ppermute(v, ('mesh', 'blk'), pairs)  6.79 us
    pallas_call x1, Pallas kernels, interp(): pl.pallas_call(functools.partial(interp_kernel, tile=tile, blocks=blocks,...  6.29 us
    ppermute x2, waiting for transfers between devices, shift(): return lax.ppermute(v, ('mesh', 'blk'), pairs)  4.11 us
    ppermute x1, starting transfers between devices, local(): lax.ppermute(low, 'blk', [((i + 1) % blocks, i) for i in range(blocks)])  4.06 us
    pallas_call x1, Pallas kernels, march(): pl.pallas_call(march_kernel, out_shape=(jax.ShapeDtypeStruct((nf * npl, n...  3.5 us
    pallas_call x1, Pallas kernels, finish(): pl.pallas_call(functools.partial(finish_kernel, edges=len(e) == 2, blocks...  3.37 us
  transfers between devices with their start and end apart: 6, of which 2 were waited for; matrix products, arithmetic and copies ran while one was open for 0% of the time, Pallas kernels for 32%

profile of v4, /device:TPU:1, one launch (start us, length us, event | category | flops | bytes accessed | tf_op | source)
XLA Modules:
  0.0 53.5 jit_solution(14830264245527972486)
XLA Ops:
  0.0 2.3 %pack.1 = (f32[352,128]{1,0:T(8,128)}, f32[352,128]{1,0:T(8,128)}) custom-call(f32[4,128,256]{2,1,0:T(8,128)} %bitcast.43, f32[2,128,256]{2,1,0:T(8,128)} %bitcast.46, f32[128,256]{1,0:T(8,128)} %bitcast.48), custom_call_target="tpu_custom_call" | custom-call | tf_op jit(solution)/shard_map/pack/pallas_call | solution.py:169
  2.3 2.1 %collective-permute-start.14 = (f32[352,128]{1,0:T(8,128)}, f32[352,128]{1,0:T(8,128)S(1)}, u32[]{:S(2)}, u32[]{:S(2)}) collective-permute-start(f32[352,128]{1,0:T(8,128)} %get-tuple-element.199.hi_ref), channel_id=1, source_target_pairs={{0,1},{1,2},{2,3},{3,4},{4,5},{5,6},{6,7},{7,8},{8,9},{9,10},{10,1... | collective-permute-start | bytes 540680 | tf_op jit(solution)/shard_map/ppermute | solution.py:642
  4.4 4.1 %collective-permute-start.15 = (f32[352,128]{1,0:T(8,128)}, f32[352,128]{1,0:T(8,128)S(1)}, u32[]{:S(2)}, u32[]{:S(2)}) collective-permute-start(f32[352,128]{1,0:T(8,128)} %get-tuple-element.200.lo_ref), channel_id=1, source_target_pairs={{1,0},{2,1},{3,2},{4,3},{5,4},{6,5},{7,6},{8,7},{9,8},{10,9},{11,1... | collective-permute-start | bytes 540680 | tf_op jit(solution)/shard_map/ppermute | solution.py:643
  9.1 0.0 copy-start
  9.1 1.0 %copy-done = f32[1,1,4,128,256]{4,3,2,1,0:T(8,128)S(1)} copy-done((f32[1,1,4,128,256]{4,3,2,1,0:T(8,128)S(1)}, f32[1,1,4,128,256]{4,3,2,1,0:T(8,128)}, u32[]{:S(2)}) %copy-start) | copy-done | bytes 524312
  10.2 0.0 copy-start.1
  10.2 0.0 copy-start.3
  10.2 0.0 copy-start.7
  10.2 6.3 %interp.1 = f32[32,8,128]{2,1,0:T(8,128)} custom-call(s32[1]{0:T(128)S(6)} %copy.43.turn_any.turn_ref, f32[4,128,256]{2,1,0:T(8,128)S(1)} %bitcast.44, s32[1,4096]{1,0:T(1,128)} %bitcast.66, f32[3,1,4096]{2,1,0:T(1,128)} %bitcast.50), custom_call_target="tpu_custom_call" | custom-call | tf_op jit(solution)/shard_map/interp/pallas_call | solution.py:261
  16.5 0.0 copy-start.2
  16.5 0.0 collective-permute-done.14.left_ref
  16.5 0.0 collective-permute-done.15.right_ref
  16.5 3.3 %all-to-all-start.7 = ((f32[32,8,128]{2,1,0:T(8,128)}), f32[32,8,128]{2,1,0:T(8,128)S(1)}, u32[]{:S(2)}, u32[]{:S(2)}) async-start(f32[32,8,128]{2,1,0:T(8,128)} %interp.1), calls=%async_computation.7 | async-start | bytes 262144 | tf_op jit(solution)/shard_map/all_to_all | solution.py:612
  19.9 0.0 copy-done.1
  19.9 0.0 copy-done.3
  19.9 0.0 copy-done.7
  19.9 0.0 copy-done.2
  19.9 0.0 copy-start.4
  19.9 0.9 %copy-done.4 = f32[352,128]{1,0:T(8,128)S(1)} copy-done((f32[352,128]{1,0:T(8,128)S(1)}, f32[352,128]{1,0:T(8,128)}, u32[]{:S(2)}) %copy-start.4) | copy-done | bytes 180248
  20.8 0.0 copy-start.5
  20.8 0.9 %copy-done.5 = f32[352,128]{1,0:T(8,128)S(1)} copy-done((f32[352,128]{1,0:T(8,128)S(1)}, f32[352,128]{1,0:T(8,128)}, u32[]{:S(2)}) %copy-start.5) | copy-done | bytes 180248
  21.7 0.0 copy-start.6
  21.7 0.0 copy-start.8
  21.7 3.5 %march.1 = (f32[1024,128]{1,0:T(8,128)S(1)}, f32[1152,128]{1,0:T(8,128)S(1)}, f32[1024,128]{1,0:T(8,128)S(1)}) custom-call(f32[4,128,256]{2,1,0:T(8,128)S(1)} %bitcast.45, f32[2,128,256]{2,1,0:T(8,128)S(1)} %bitcast.47, f32[128,256]{1,0:T(8,128)S(1)} %bitcast.49, f32[352,128]{1,0:T(8,128)S(1)} %copy-done.4, f32[352,128]{1,0:T(8,128)S(1)} %copy-done.5, ...), custom_call_target="tpu_custom_call" | custom-call | tf_op jit(solution)/shard_map/march/pallas_call | solution.py:388
  25.3 2.3 %all-to-all-done.7 = f32[32,8,128]{2,1,0:T(8,128)S(1)} async-done(((f32[32,8,128]{2,1,0:T(8,128)}), f32[32,8,128]{2,1,0:T(8,128)S(1)}, u32[]{:S(2)}, u32[]{:S(2)}) %all-to-all-start.7) | async-done | bytes 131104 | tf_op jit(solution)/shard_map/all_to_all | solution.py:612
  27.5 0.0 copy-done.6
  27.5 0.0 copy-done.8
  27.5 22.4 %conditional.1 = (f32[32,8,128]{2,1,0:T(8,128)}, f32[1152,128]{1,0:T(8,128)}, f32[64,128]{1,0:T(8,128)}, f32[64,128]{1,0:T(8,128)}) conditional(s32[]{:T(128)} %bitcast.35, (s32[1,1,4096]{2,1,0:T(1,128)S(1)}, s32[1,1,4096]{2,1,0:T(1,128)S(1)}, f32[1,1,3,4096]{3,1,2,0:T(1,128)S(1)}, s32[1]{0:T(128)}, ...), branch_computations={%region_0.0_spmd, %region_1.0_spmd, %region_2.0_spmd, %region_3.0_... | conditional | bytes 2883728 | solution.py:667
  27.5 2.6 %collective-permute-start.10 = (f32[1152,128]{1,0:T(8,128)S(1)}, f32[1152,128]{1,0:T(8,128)}, u32[]{:S(2)}, u32[]{:S(2)}) collective-permute-start(f32[1152,128]{1,0:T(8,128)S(1)} %get-tuple-element.175), channel_id=1, source_target_pairs={{16,22},{17,23},{18,24},{19,25},{20,26},{21,27},{22,28},{23,29},{2... | collective-permute-start | bytes 1769480 | tf_op jit(solution)/shard_map/cond/branch_5_fun/ppermute | solution.py:650
  30.1 7.5 %relay.12 = (f32[32,8,128]{2,1,0:T(8,128)}, f32[64,128]{1,0:T(8,128)}) custom-call(s32[1]{0:T(128)} %get-tuple-element.167.turn_ref, f32[32,8,128]{2,1,0:T(8,128)S(1)} %get-tuple-element.168.arr_ref, s32[1,4096]{1,0:T(1,128)S(1)} %bitcast.64, f32[1024,128]{1,0:T(8,128)S(1)} %get-tuple-element.170.f1t_ref, f32[1024,128]{1,0:T(8,128)S(1)} %get-tuple-element.171.fac_ref, ...), custom_call_target="tpu_custom_call" | custom-call | tf_op jit(solution)/shard_map/cond/branch_5_fun/relay/pallas_call | solution.py:478
  37.6 4.0 %all-to-all-start.5 = ((f32[32,8,128]{2,1,0:T(8,128)}), f32[32,8,128]{2,1,0:T(8,128)}, u32[]{:S(2)}, u32[]{:S(2)}) async-start(f32[32,8,128]{2,1,0:T(8,128)} %get-tuple-element.174), calls=%async_computation.5 | async-start | bytes 262144 | tf_op jit(solution)/shard_map/cond/branch_5_fun/all_to_all | solution.py:612
  41.6 4.2 %collective-permute-start.11 = (f32[64,128]{1,0:T(8,128)}, f32[64,128]{1,0:T(8,128)}, u32[]{:S(2)}, u32[]{:S(2)}) collective-permute-start(f32[64,128]{1,0:T(8,128)} %get-tuple-element.289), channel_id=1, source_target_pairs={{16,22},{17,23},{18,24},{19,25},{20,26},{21,27},{22,28},{23,29},{2... | collective-permute-start | bytes 98312 | tf_op jit(solution)/shard_map/cond/branch_5_fun/ppermute | solution.py:650
  45.8 4.1 %collective-permute-done.11 = f32[64,128]{1,0:T(8,128)} collective-permute-done((f32[64,128]{1,0:T(8,128)}, f32[64,128]{1,0:T(8,128)}, u32[]{:S(2)}, u32[]{:S(2)}) %collective-permute-start.11) | collective-permute-done | bytes 32800 | tf_op jit(solution)/shard_map/cond/branch_5_fun/ppermute | solution.py:650
  49.9 0.0 all-to-all-done.5
  49.9 0.0 collective-permute-done.10
  49.9 3.4 %finish.1 = f32[4,128,256]{2,1,0:T(8,128)} custom-call(s32[1]{0:T(128)S(6)} %copy.43.turn_any.turn_ref, f32[32,8,128]{2,1,0:T(8,128)} %get-tuple-element.207.arr_any, f32[1152,128]{1,0:T(8,128)S(1)} %get-tuple-element.206.own_ref, f32[1152,128]{1,0:T(8,128)} %get-tuple-element.208.moved_ref, f32[64,128]{1,0:T(8,128)} %get-tuple-element.209.e_any, ...), custom_call_target="tpu_custom_call" | custom-call | tf_op jit(solution)/shard_map/finish/pallas_call | solution.py:594
Async XLA Ops:
  2.3 14.2 %collective-permute-start.14 = (f32[352,128]{1,0:T(8,128)}, f32[352,128]{1,0:T(8,128)S(1)}, u32[]{:S(2)}, u32[]{:S(2)}) collective-permute-start(f32[352,128]{1,0:T(8,128)} %get-tuple-element.199.hi_ref), channel_id=1, source_target_pairs={{0,1},{1,2},{2,3},{3,4},{4,5},{5,6},{6,7},{7,8},{8,9},{9,10},{10,1... | collective-permute-start | bytes 540680 | tf_op jit(solution)/shard_map/ppermute | solution.py:642
  4.4 12.1 %collective-permute-start.15 = (f32[352,128]{1,0:T(8,128)}, f32[352,128]{1,0:T(8,128)S(1)}, u32[]{:S(2)}, u32[]{:S(2)}) collective-permute-start(f32[352,128]{1,0:T(8,128)} %get-tuple-element.200.lo_ref), channel_id=1, source_target_pairs={{1,0},{2,1},{3,2},{4,3},{5,4},{6,5},{7,6},{8,7},{9,8},{10,9},{11,1... | collective-permute-start | bytes 540680 | tf_op jit(solution)/shard_map/ppermute | solution.py:643
  9.1 1.0 %copy-start = (f32[1,1,4,128,256]{4,3,2,1,0:T(8,128)S(1)}, f32[1,1,4,128,256]{4,3,2,1,0:T(8,128)}, u32[]{:S(2)}) copy-start(f32[1,1,4,128,256]{4,3,2,1,0:T(8,128)} %param.15) | copy-start | bytes 1572868
  10.2 9.7 %copy-start.1 = (f32[1,1,4,128,256]{4,3,2,1,0:T(8,128)S(1)}, f32[1,1,4,128,256]{4,3,2,1,0:T(8,128)}, u32[]{:S(2)}) copy-start(f32[1,1,4,128,256]{4,3,2,1,0:T(8,128)} %param.15) | copy-start | bytes 1572868
  10.2 9.7 %copy-start.3 = (f32[1,1,128,256]{3,2,1,0:T(8,128)S(1)}, f32[1,1,128,256]{3,2,1,0:T(8,128)}, u32[]{:S(2)}) copy-start(f32[1,1,128,256]{3,2,1,0:T(8,128)} %param.17) | copy-start | bytes 393220
  10.2 9.7 %copy-start.7 = (s32[1,1,4096]{2,1,0:T(1,128)S(1)}, s32[1,1,4096]{2,1,0:T(1,128)}, u32[]{:S(2)}) copy-start(s32[1,1,4096]{2,1,0:T(1,128)} %param.20) | copy-start | bytes 49156
  16.5 3.4 %copy-start.2 = (f32[1,1,2,128,256]{4,3,2,1,0:T(8,128)S(1)}, f32[1,1,2,128,256]{4,3,2,1,0:T(8,128)}, u32[]{:S(2)}) copy-start(f32[1,1,2,128,256]{4,3,2,1,0:T(8,128)} %param.16) | copy-start | bytes 786436
  16.5 11.0 %all-to-all-start.7 = ((f32[32,8,128]{2,1,0:T(8,128)}), f32[32,8,128]{2,1,0:T(8,128)S(1)}, u32[]{:S(2)}, u32[]{:S(2)}) async-start(f32[32,8,128]{2,1,0:T(8,128)} %interp.1), calls=%async_computation.7 | async-start | bytes 262144 | tf_op jit(solution)/shard_map/all_to_all | solution.py:612
  19.9 0.9 %copy-start.4 = (f32[352,128]{1,0:T(8,128)S(1)}, f32[352,128]{1,0:T(8,128)}, u32[]{:S(2)}) copy-start(f32[352,128]{1,0:T(8,128)} %get-tuple-element.200.lo_ref) | copy-start | bytes 540676
  20.8 0.9 %copy-start.5 = (f32[352,128]{1,0:T(8,128)S(1)}, f32[352,128]{1,0:T(8,128)}, u32[]{:S(2)}) copy-start(f32[352,128]{1,0:T(8,128)} %get-tuple-element.199.hi_ref) | copy-start | bytes 540676
  21.7 5.8 %copy-start.6 = (f32[1,1,3,4096]{3,1,2,0:T(1,128)S(1)}, f32[1,1,3,4096]{3,1,2,0:T(1,128)}, u32[]{:S(2)}) copy-start(f32[1,1,3,4096]{3,1,2,0:T(1,128)} %param.19) | copy-start | bytes 147460
  21.7 5.8 %copy-start.8 = (s32[1,1,4096]{2,1,0:T(1,128)S(1)}, s32[1,1,4096]{2,1,0:T(1,128)}, u32[]{:S(2)}) copy-start(s32[1,1,4096]{2,1,0:T(1,128)} %param.18) | copy-start | bytes 49156
  27.5 22.4 %collective-permute-start.10 = (f32[1152,128]{1,0:T(8,128)S(1)}, f32[1152,128]{1,0:T(8,128)}, u32[]{:S(2)}, u32[]{:S(2)}) collective-permute-start(f32[1152,128]{1,0:T(8,128)S(1)} %get-tuple-element.175), channel_id=1, source_target_pairs={{16,22},{17,23},{18,24},{19,25},{20,26},{21,27},{22,28},{23,29},{2... | collective-permute-start | bytes 1769480 | tf_op jit(solution)/shard_map/cond/branch_5_fun/ppermute | solution.py:650
  37.6 12.3 %all-to-all-start.5 = ((f32[32,8,128]{2,1,0:T(8,128)}), f32[32,8,128]{2,1,0:T(8,128)}, u32[]{:S(2)}, u32[]{:S(2)}) async-start(f32[32,8,128]{2,1,0:T(8,128)} %get-tuple-element.174), calls=%async_computation.5 | async-start | bytes 262144 | tf_op jit(solution)/shard_map/cond/branch_5_fun/all_to_all | solution.py:612
  41.6 8.3 %collective-permute-start.11 = (f32[64,128]{1,0:T(8,128)}, f32[64,128]{1,0:T(8,128)}, u32[]{:S(2)}, u32[]{:S(2)}) collective-permute-start(f32[64,128]{1,0:T(8,128)} %get-tuple-element.289), channel_id=1, source_target_pairs={{16,22},{17,23},{18,24},{19,25},{20,26},{21,27},{22,28},{23,29},{2... | collective-permute-start | bytes 98312 | tf_op jit(solution)/shard_map/cond/branch_5_fun/ppermute | solution.py:650

commit v5 on v3

--- a/solution.py
+++ b/solution.py
@@ -241,18 +241,19 @@
         a_ref[row:row + n, i * nz:(i + 1) * nz] = part
 
 
-def interp_kernel(turn_any, f_ref, base_any, frac_any, o_ref, a_ref, base_ref, frac_ref, turn_ref, sems, *, tile, blocks, turned):
+def interp_kernel(turn_any, f_ref, base_any, frac_any, o_ref, a_ref, t_ref, base_ref, frac_ref, turn_ref, sems, *, tile, blocks, turned):
     nf, nz, npl = f_ref.shape
     pairs = ((base_any, base_ref), (frac_any, frac_ref), (turn_any, turn_ref))
     copies = [pltpu.make_async_copy(a, b, sems.at[i]) for i, (a, b) in enumerate(pairs)]
     for c in copies:
         c.start()
-    for f in range(nf):
+    for f in range(nf - 1):
         split_into(a_ref, f * npl, f_ref[f].T)
+    t_ref[...] = f_ref[nf - 1].T
     for c in copies:
         c.wait()
     info_ref = places(turn_ref[0], base_ref.shape[1] // tile, blocks, turned)
-    load_tiles(16, o_ref, info_ref, base_ref, frac_ref, a_ref, info_ref[0], nf, nz, npl, tile)
+    load_tiles(16, o_ref, info_ref, base_ref, frac_ref, a_ref, info_ref[0], nf, nz, npl, tile, t_ref)
 
 
 def interp(turn, fields, base, frac, tile, blocks, turned):
@@ -263,7 +264,7 @@
         out_shape=jax.ShapeDtypeStruct((2 * slots // tile, nf * tile // 128, 128), F32),
         in_specs=[ANY, VM, ANY, ANY],
         out_specs=VM,
-        scratch_shapes=[pltpu.VMEM((nf * npl, 4 * nz), BF),
+        scratch_shapes=[pltpu.VMEM((nf * npl, 4 * nz), BF), pltpu.VMEM((npl, nz), F32),
                         pltpu.VMEM(base.shape, jnp.int32), pltpu.VMEM(frac.shape, F32),
                         pltpu.SMEM((1,), jnp.int32), pltpu.SemaphoreType.DMA((3,))],
         compiler_params=CP,

time: 54.5 us -> 54.7 us (level)
  starting transfers between devices: 20.2 us -> 21.3 us
    all_to_all x2, starting transfers between devices: 7.31 us -> 8.64 us  [exchange(): return lax.all_to_all(values, ('mesh', 'blk'), 0, 0, tiled=True)]
where the time goes in v5:
time: 54.7 us; the launch traced here: 54.2 us
  Pallas kernels  22.7 us (41%)
  starting transfers between devices  21.3 us (39%)
  waiting for transfers between devices  6.39 us (12%)
  local copies, waits for them, and re-layouts  2.9 us (5%)
  between operations  0.95 us (2%)
    all_to_all x2, starting transfers between devices, exchange(): return lax.all_to_all(values, ('mesh', 'blk'), 0, 0, tiled=True)  8.64 us
    pallas_call x1, Pallas kernels, relay(): pl.pallas_call(functools.partial(relay_kernel, tile=tile, nf=nf, edges=ed...  7.45 us
    ppermute x2, starting transfers between devices, shift(): return lax.ppermute(v, ('mesh', 'blk'), pairs)  6.47 us
    pallas_call x1, Pallas kernels, interp(): pl.pallas_call(functools.partial(interp_kernel, tile=tile, blocks=blocks,...  6.17 us
    ppermute x2, waiting for transfers between devices, shift(): return lax.ppermute(v, ('mesh', 'blk'), pairs)  4.17 us
    ppermute x1, starting transfers between devices, local(): lax.ppermute(low, 'blk', [((i + 1) % blocks, i) for i in range(blocks)])  4.06 us
    pallas_call x1, Pallas kernels, march(): pl.pallas_call(march_kernel, out_shape=(jax.ShapeDtypeStruct((nf * npl, n...  3.49 us
    pallas_call x1, Pallas kernels, finish(): pl.pallas_call(functools.partial(finish_kernel, edges=len(e) == 2, blocks...  3.24 us
  transfers between devices with their start and end apart: 6, of which 2 were waited for; matrix products, arithmetic and copies ran while one was open for 0% of the time, Pallas kernels for 32%

profile of v5, /device:TPU:1, one launch (start us, length us, event | category | flops | bytes accessed | tf_op | source)
XLA Modules:
  0.0 54.2 jit_solution(16125437919990708889)
XLA Ops:
  0.0 2.3 %pack.1 = (f32[352,128]{1,0:T(8,128)}, f32[352,128]{1,0:T(8,128)}) custom-call(f32[4,128,256]{2,1,0:T(8,128)} %bitcast.43, f32[2,128,256]{2,1,0:T(8,128)} %bitcast.46, f32[128,256]{1,0:T(8,128)} %bitcast.48), custom_call_target="tpu_custom_call" | custom-call | tf_op jit(solution)/shard_map/pack/pallas_call | solution.py:169
  2.3 2.1 %collective-permute-start.14 = (f32[352,128]{1,0:T(8,128)}, f32[352,128]{1,0:T(8,128)S(1)}, u32[]{:S(2)}, u32[]{:S(2)}) collective-permute-start(f32[352,128]{1,0:T(8,128)} %get-tuple-element.199.hi_ref), channel_id=1, source_target_pairs={{0,1},{1,2},{2,3},{3,4},{4,5},{5,6},{6,7},{7,8},{8,9},{9,10},{10,1... | collective-permute-start | bytes 540680 | tf_op jit(solution)/shard_map/ppermute | solution.py:638
  4.4 4.1 %collective-permute-start.15 = (f32[352,128]{1,0:T(8,128)}, f32[352,128]{1,0:T(8,128)S(1)}, u32[]{:S(2)}, u32[]{:S(2)}) collective-permute-start(f32[352,128]{1,0:T(8,128)} %get-tuple-element.200.lo_ref), channel_id=1, source_target_pairs={{1,0},{2,1},{3,2},{4,3},{5,4},{6,5},{7,6},{8,7},{9,8},{10,9},{11,1... | collective-permute-start | bytes 540680 | tf_op jit(solution)/shard_map/ppermute | solution.py:639
  9.1 0.0 copy-start
  9.1 1.0 %copy-done = f32[1,1,4,128,256]{4,3,2,1,0:T(8,128)S(1)} copy-done((f32[1,1,4,128,256]{4,3,2,1,0:T(8,128)S(1)}, f32[1,1,4,128,256]{4,3,2,1,0:T(8,128)}, u32[]{:S(2)}) %copy-start) | copy-done | bytes 524312
  10.2 0.0 copy-start.1
  10.2 0.0 copy-start.3
  10.2 0.0 copy-start.7
  10.2 6.2 %interp.1 = f32[32,8,128]{2,1,0:T(8,128)} custom-call(s32[1]{0:T(128)S(6)} %copy.43.turn_any.turn_ref, f32[4,128,256]{2,1,0:T(8,128)S(1)} %bitcast.44, s32[1,4096]{1,0:T(1,128)} %bitcast.66, f32[3,1,4096]{2,1,0:T(1,128)} %bitcast.50), custom_call_target="tpu_custom_call" | custom-call | tf_op jit(solution)/shard_map/interp/pallas_call | solution.py:262
  16.4 0.0 copy-start.2
  16.4 0.0 collective-permute-done.14.left_ref
  16.4 0.0 collective-permute-done.15.right_ref
  16.4 3.4 %all-to-all-start.7 = ((f32[32,8,128]{2,1,0:T(8,128)}), f32[32,8,128]{2,1,0:T(8,128)S(1)}, u32[]{:S(2)}, u32[]{:S(2)}) async-start(f32[32,8,128]{2,1,0:T(8,128)} %interp.1), calls=%async_computation.7 | async-start | bytes 262144 | tf_op jit(solution)/shard_map/all_to_all | solution.py:608
  19.9 0.0 copy-done.1
  19.9 0.0 copy-done.3
  19.9 0.0 copy-done.7
  19.9 0.0 copy-done.2
  19.9 0.0 copy-start.4
  19.9 0.9 %copy-done.4 = f32[352,128]{1,0:T(8,128)S(1)} copy-done((f32[352,128]{1,0:T(8,128)S(1)}, f32[352,128]{1,0:T(8,128)}, u32[]{:S(2)}) %copy-start.4) | copy-done | bytes 180248
  20.8 0.0 copy-start.5
  20.8 0.9 %copy-done.5 = f32[352,128]{1,0:T(8,128)S(1)} copy-done((f32[352,128]{1,0:T(8,128)S(1)}, f32[352,128]{1,0:T(8,128)}, u32[]{:S(2)}) %copy-start.5) | copy-done | bytes 180248
  21.7 0.0 copy-start.6
  21.7 0.0 copy-start.8
  21.7 3.5 %march.1 = (f32[1024,128]{1,0:T(8,128)S(1)}, f32[1184,128]{1,0:T(8,128)S(1)}, f32[1024,128]{1,0:T(8,128)S(1)}) custom-call(f32[4,128,256]{2,1,0:T(8,128)S(1)} %bitcast.45, f32[2,128,256]{2,1,0:T(8,128)S(1)} %bitcast.47, f32[128,256]{1,0:T(8,128)S(1)} %bitcast.49, f32[352,128]{1,0:T(8,128)S(1)} %copy-done.4, f32[352,128]{1,0:T(8,128)S(1)} %copy-done.5, ...), custom_call_target="tpu_custom_call" | custom-call | tf_op jit(solution)/shard_map/march/pallas_call | solution.py:386
  25.2 2.2 %all-to-all-done.7 = f32[32,8,128]{2,1,0:T(8,128)S(1)} async-done(((f32[32,8,128]{2,1,0:T(8,128)}), f32[32,8,128]{2,1,0:T(8,128)S(1)}, u32[]{:S(2)}, u32[]{:S(2)}) %all-to-all-start.7) | async-done | bytes 131104 | tf_op jit(solution)/shard_map/all_to_all | solution.py:608
  27.5 0.0 copy-done.6
  27.5 0.0 copy-done.8
  27.5 23.3 %conditional.1 = (f32[32,8,128]{2,1,0:T(8,128)}, f32[1184,128]{1,0:T(8,128)}, f32[64,128]{1,0:T(8,128)}, f32[64,128]{1,0:T(8,128)}) conditional(s32[]{:T(128)} %bitcast.35, (s32[1,1,4096]{2,1,0:T(1,128)S(1)}, s32[1,1,4096]{2,1,0:T(1,128)S(1)}, f32[1,1,3,4096]{3,1,2,0:T(1,128)S(1)}, s32[1]{0:T(128)}, ...), branch_computations={%region_0.0_spmd, %region_1.0_spmd, %region_2.0_spmd, %region_3.0_... | conditional | bytes 2949264 | solution.py:663
  27.5 2.3 %collective-permute-start.8 = (f32[1184,128]{1,0:T(8,128)S(1)}, f32[1184,128]{1,0:T(8,128)}, u32[]{:S(2)}, u32[]{:S(2)}) collective-permute-start(f32[1184,128]{1,0:T(8,128)S(1)} %get-tuple-element.165), channel_id=1, source_target_pairs={{16,21},{17,22},{18,23},{19,24},{20,25},{21,26},{22,27},{23,28},{2... | collective-permute-start | bytes 1818632 | tf_op jit(solution)/shard_map/cond/branch_4_fun/ppermute | solution.py:646
  29.7 7.5 %relay.11 = (f32[32,8,128]{2,1,0:T(8,128)}, f32[64,128]{1,0:T(8,128)}) custom-call(s32[1]{0:T(128)} %get-tuple-element.157.turn_ref, f32[32,8,128]{2,1,0:T(8,128)S(1)} %get-tuple-element.158.arr_ref, s32[1,4096]{1,0:T(1,128)S(1)} %bitcast.63, f32[1024,128]{1,0:T(8,128)S(1)} %get-tuple-element.160.f1t_ref, f32[1024,128]{1,0:T(8,128)S(1)} %get-tuple-element.161.fac_ref, ...), custom_call_target="tpu_custom_call" | custom-call | tf_op jit(solution)/shard_map/cond/branch_4_fun/relay/pallas_call | solution.py:476
  37.2 5.2 %all-to-all-start.4 = ((f32[32,8,128]{2,1,0:T(8,128)}), f32[32,8,128]{2,1,0:T(8,128)}, u32[]{:S(2)}, u32[]{:S(2)}) async-start(f32[32,8,128]{2,1,0:T(8,128)} %get-tuple-element.164), calls=%async_computation.4 | async-start | bytes 262144 | tf_op jit(solution)/shard_map/cond/branch_4_fun/all_to_all | solution.py:608
  42.4 4.2 %collective-permute-start.9 = (f32[64,128]{1,0:T(8,128)}, f32[64,128]{1,0:T(8,128)}, u32[]{:S(2)}, u32[]{:S(2)}) collective-permute-start(f32[64,128]{1,0:T(8,128)} %get-tuple-element.285), channel_id=1, source_target_pairs={{16,21},{17,22},{18,23},{19,24},{20,25},{21,26},{22,27},{23,28},{2... | collective-permute-start | bytes 98312 | tf_op jit(solution)/shard_map/cond/branch_4_fun/ppermute | solution.py:646
  46.6 4.2 %collective-permute-done.9 = f32[64,128]{1,0:T(8,128)} collective-permute-done((f32[64,128]{1,0:T(8,128)}, f32[64,128]{1,0:T(8,128)}, u32[]{:S(2)}, u32[]{:S(2)}) %collective-permute-start.9) | collective-permute-done | bytes 32800 | tf_op jit(solution)/shard_map/cond/branch_4_fun/ppermute | solution.py:646
  50.8 0.0 all-to-all-done.4
  50.8 0.0 collective-permute-done.8
  50.8 3.2 %finish.1 = f32[4,128,256]{2,1,0:T(8,128)} custom-call(s32[1]{0:T(128)S(6)} %copy.43.turn_any.turn_ref, f32[32,8,128]{2,1,0:T(8,128)} %get-tuple-element.207.arr_any, f32[1184,128]{1,0:T(8,128)S(1)} %get-tuple-element.206.own_ref, f32[1184,128]{1,0:T(8,128)} %get-tuple-element.208.moved_ref, f32[64,128]{1,0:T(8,128)} %get-tuple-element.209.e_any, ...), custom_call_target="tpu_custom_call" | custom-call | tf_op jit(solution)/shard_map/finish/pallas_call | solution.py:590
Async XLA Ops:
  2.3 14.1 %collective-permute-start.14 = (f32[352,128]{1,0:T(8,128)}, f32[352,128]{1,0:T(8,128)S(1)}, u32[]{:S(2)}, u32[]{:S(2)}) collective-permute-start(f32[352,128]{1,0:T(8,128)} %get-tuple-element.199.hi_ref), channel_id=1, source_target_pairs={{0,1},{1,2},{2,3},{3,4},{4,5},{5,6},{6,7},{7,8},{8,9},{9,10},{10,1... | collective-permute-start | bytes 540680 | tf_op jit(solution)/shard_map/ppermute | solution.py:638
  4.4 12.0 %collective-permute-start.15 = (f32[352,128]{1,0:T(8,128)}, f32[352,128]{1,0:T(8,128)S(1)}, u32[]{:S(2)}, u32[]{:S(2)}) collective-permute-start(f32[352,128]{1,0:T(8,128)} %get-tuple-element.200.lo_ref), channel_id=1, source_target_pairs={{1,0},{2,1},{3,2},{4,3},{5,4},{6,5},{7,6},{8,7},{9,8},{10,9},{11,1... | collective-permute-start | bytes 540680 | tf_op jit(solution)/shard_map/ppermute | solution.py:639
  9.1 1.0 %copy-start = (f32[1,1,4,128,256]{4,3,2,1,0:T(8,128)S(1)}, f32[1,1,4,128,256]{4,3,2,1,0:T(8,128)}, u32[]{:S(2)}) copy-start(f32[1,1,4,128,256]{4,3,2,1,0:T(8,128)} %param.15) | copy-start | bytes 1572868
  10.2 9.7 %copy-start.1 = (f32[1,1,4,128,256]{4,3,2,1,0:T(8,128)S(1)}, f32[1,1,4,128,256]{4,3,2,1,0:T(8,128)}, u32[]{:S(2)}) copy-start(f32[1,1,4,128,256]{4,3,2,1,0:T(8,128)} %param.15) | copy-start | bytes 1572868
  10.2 9.7 %copy-start.3 = (f32[1,1,128,256]{3,2,1,0:T(8,128)S(1)}, f32[1,1,128,256]{3,2,1,0:T(8,128)}, u32[]{:S(2)}) copy-start(f32[1,1,128,256]{3,2,1,0:T(8,128)} %param.17) | copy-start | bytes 393220
  10.2 9.7 %copy-start.7 = (s32[1,1,4096]{2,1,0:T(1,128)S(1)}, s32[1,1,4096]{2,1,0:T(1,128)}, u32[]{:S(2)}) copy-start(s32[1,1,4096]{2,1,0:T(1,128)} %param.20) | copy-start | bytes 49156
  16.4 3.5 %copy-start.2 = (f32[1,1,2,128,256]{4,3,2,1,0:T(8,128)S(1)}, f32[1,1,2,128,256]{4,3,2,1,0:T(8,128)}, u32[]{:S(2)}) copy-start(f32[1,1,2,128,256]{4,3,2,1,0:T(8,128)} %param.16) | copy-start | bytes 786436
  16.4 11.1 %all-to-all-start.7 = ((f32[32,8,128]{2,1,0:T(8,128)}), f32[32,8,128]{2,1,0:T(8,128)S(1)}, u32[]{:S(2)}, u32[]{:S(2)}) async-start(f32[32,8,128]{2,1,0:T(8,128)} %interp.1), calls=%async_computation.7 | async-start | bytes 262144 | tf_op jit(solution)/shard_map/all_to_all | solution.py:608
  19.9 0.9 %copy-start.4 = (f32[352,128]{1,0:T(8,128)S(1)}, f32[352,128]{1,0:T(8,128)}, u32[]{:S(2)}) copy-start(f32[352,128]{1,0:T(8,128)} %get-tuple-element.200.lo_ref) | copy-start | bytes 540676
  20.8 0.9 %copy-start.5 = (f32[352,128]{1,0:T(8,128)S(1)}, f32[352,128]{1,0:T(8,128)}, u32[]{:S(2)}) copy-start(f32[352,128]{1,0:T(8,128)} %get-tuple-element.199.hi_ref) | copy-start | bytes 540676
  21.7 5.7 %copy-start.6 = (f32[1,1,3,4096]{3,1,2,0:T(1,128)S(1)}, f32[1,1,3,4096]{3,1,2,0:T(1,128)}, u32[]{:S(2)}) copy-start(f32[1,1,3,4096]{3,1,2,0:T(1,128)} %param.19) | copy-start | bytes 147460
  21.7 5.7 %copy-start.8 = (s32[1,1,4096]{2,1,0:T(1,128)S(1)}, s32[1,1,4096]{2,1,0:T(1,128)}, u32[]{:S(2)}) copy-start(s32[1,1,4096]{2,1,0:T(1,128)} %param.18) | copy-start | bytes 49156
  27.5 23.3 %collective-permute-start.8 = (f32[1184,128]{1,0:T(8,128)S(1)}, f32[1184,128]{1,0:T(8,128)}, u32[]{:S(2)}, u32[]{:S(2)}) collective-permute-start(f32[1184,128]{1,0:T(8,128)S(1)} %get-tuple-element.165), channel_id=1, source_target_pairs={{16,21},{17,22},{18,23},{19,24},{20,25},{21,26},{22,27},{23,28},{2... | collective-permute-start | bytes 1818632 | tf_op jit(solution)/shard_map/cond/branch_4_fun/ppermute | solution.py:646
  37.2 13.6 %all-to-all-start.4 = ((f32[32,8,128]{2,1,0:T(8,128)}), f32[32,8,128]{2,1,0:T(8,128)}, u32[]{:S(2)}, u32[]{:S(2)}) async-start(f32[32,8,128]{2,1,0:T(8,128)} %get-tuple-element.164), calls=%async_computation.4 | async-start | bytes 262144 | tf_op jit(solution)/shard_map/cond/branch_4_fun/all_to_all | solution.py:608
  42.4 8.4 %collective-permute-start.9 = (f32[64,128]{1,0:T(8,128)}, f32[64,128]{1,0:T(8,128)}, u32[]{:S(2)}, u32[]{:S(2)}) collective-permute-start(f32[64,128]{1,0:T(8,128)} %get-tuple-element.285), channel_id=1, source_target_pairs={{16,21},{17,22},{18,23},{19,24},{20,25},{21,26},{22,27},{23,28},{2... | collective-permute-start | bytes 98312 | tf_op jit(solution)/shard_map/cond/branch_4_fun/ppermute | solution.py:646
